TPU v7x, 32 devices: a whole 2x2x4 slice. The times are simulated.
32 devices in a mesh: enc: 16 (over z, y, x), dec: 2 (over core).
Axes of the slice: x: 2, y: 2, z: 4, core: 2. Of those that a mesh axis runs over, the one named last changes fastest.
Arguments:
- pixels: bfloat16 [2, 144, 3072], P('dec', 'enc'), may hold values from -6 to 6
- tile_counts: int32 [2, 16], P('dec', 'enc'), may hold values from 1 to 9, as said below
- text_gaps: int32 [2, 16], P('dec', 'enc'), may hold values from 0 to 64
- stem_weight: bfloat16 [48, 384], replicated, may hold values from -0.875 to 0.875
- depth_weight: bfloat16 [49, 384], replicated, may hold values from -0.875 to 0.875
- norm_gain: float32 [384], replicated, may hold values from 0.5 to 2
- up_weight: bfloat16 [384, 768], replicated, may hold values from -0.3125 to 0.3125
- down_weight: bfloat16 [768, 384], replicated, may hold values from -0.21875 to 0.21875
- layer_scale: float32 [384], replicated, may hold values from 0.25 to 1
- embed_grad: bfloat16 [16, 416, 384], P('enc', 'dec'), may hold values from -6 to 6
Outputs:
- image_embeds: bfloat16 [16, 416, 384], P('enc', 'dec')
- stem_grad: float32 [48, 384], replicated
- depth_grad: float32 [49, 384], replicated
- gain_grad: float32 [384], replicated
- up_grad: float32 [384, 768], replicated
- down_grad: float32 [768, 384], replicated
- scale_grad: float32 [384], replicated
Inputs may be any that keep to these rules, and one draw needn't show every extreme that they name: `tile_counts`: for each index of dec, the counts of each aligned group of four consecutive indices of enc sum to exactly 12.
All inputs are finite; a program needn't handle non-finite values.
Results may differ from a plain program's by a relative error of at most 0.013.
Values may be sent and summed in bfloat16 or wider, within the bound.
A program may use at most 64 MiB of HBM per device.

v0:
```python
import math

import jax
import jax.numpy as jnp
from jax import lax
from jax.sharding import PartitionSpec as P

WIDTH = 384
KERNEL = 7
PATCH_CH = 48
TILE = 8
MEAN_TILES = 3
SLOTS = 9
FEAT_TILE = 16


epsilon = 1e-06


def encode(tile_block, stem_weight, depth_weight, norm_gain, up_weight, down_weight, layer_scale):
    tile_total = tile_block.shape[0]
    reach = KERNEL // 2
    half_tile = TILE // 2
    patches = tile_block.reshape(tile_total * TILE * TILE, PATCH_CH)
    stem_out = jnp.dot(patches, stem_weight, preferred_element_type=jnp.float32).astype(
        jnp.bfloat16
    )
    stem_grid = stem_out.reshape(tile_total, TILE, TILE, WIDTH).astype(jnp.float32)
    padded = jnp.pad(stem_grid, ((0, 0), (reach, reach), (reach, reach), (0, 0)))
    kernel = depth_weight.astype(jnp.float32)
    mixed_field = jnp.zeros_like(stem_grid)
    for row_tap in range(KERNEL):
        for col_tap in range(KERNEL):
            mixed_field = (
                mixed_field
                + padded[:, row_tap : row_tap + TILE, col_tap : col_tap + TILE, :]
                * kernel[row_tap * KERNEL + col_tap]
            )
    flat_rows = mixed_field.reshape(-1, WIDTH)
    channel_mean = jnp.mean(flat_rows, axis=1, keepdims=True)
    deviation = flat_rows - channel_mean
    variance = jnp.mean(deviation * deviation, axis=1, keepdims=True)
    inv_std = lax.rsqrt(variance + epsilon)
    centred = deviation * inv_std
    normed = (centred * norm_gain).astype(jnp.bfloat16)
    hidden = jnp.dot(normed, up_weight, preferred_element_type=jnp.float32)
    activated = jax.nn.gelu(hidden).astype(jnp.bfloat16)
    projected = jnp.dot(activated, down_weight, preferred_element_type=jnp.float32)
    block_out = stem_grid.reshape(-1, WIDTH) + layer_scale * projected
    pooled = jnp.mean(block_out.reshape(tile_total, half_tile, 2, half_tile, 2, WIDTH), axis=(2, 4))
    pooled = pooled.reshape(tile_total, half_tile * half_tile, WIDTH)
    stored = (patches, padded, centred, inv_std, normed, hidden, activated, projected)
    return (pooled, stored)


def backward_head(stored, cotangent, down_weight, layer_scale):
    patches, padded, centred, inv_std, normed, hidden, activated, projected = stored
    tile_total = cotangent.shape[0]
    half_tile = TILE // 2
    spread_out = jnp.broadcast_to(
        cotangent.reshape(tile_total, half_tile, 1, half_tile, 1, WIDTH),
        (tile_total, half_tile, 2, half_tile, 2, WIDTH),
    )
    grad_block = (0.25 * spread_out).reshape(-1, WIDTH)
    scale_term = jnp.sum(grad_block * projected, axis=0)
    grad_proj = (grad_block * layer_scale).astype(jnp.bfloat16)
    down_term = lax.dot_general(
        activated, grad_proj, (((0,), (0,)), ((), ())), preferred_element_type=jnp.float32
    )
    grad_act = lax.dot_general(
        grad_proj, down_weight, (((1,), (1,)), ((), ())), preferred_element_type=jnp.float32
    )
    grad_hidden = jax.vjp(jax.nn.gelu, hidden)[1](grad_act)[0].astype(jnp.bfloat16)
    return (scale_term, down_term, grad_hidden, grad_block)


def backward_middle(stored, grad_hidden, up_weight, norm_gain):
    patches, padded, centred, inv_std, normed, hidden, activated, projected = stored
    up_term = lax.dot_general(
        normed, grad_hidden, (((0,), (0,)), ((), ())), preferred_element_type=jnp.float32
    )
    grad_normed = lax.dot_general(
        grad_hidden, up_weight, (((1,), (1,)), ((), ())), preferred_element_type=jnp.float32
    )
    gain_term = jnp.sum(grad_normed * centred, axis=0)
    scaled = grad_normed * norm_gain
    grad_mixed = inv_std * (
        scaled
        - jnp.mean(scaled, axis=1, keepdims=True)
        - centred * jnp.mean(scaled * centred, axis=1, keepdims=True)
    )
    return (gain_term, up_term, grad_mixed)


def backward_tail(stored, grad_mixed, grad_block, depth_weight):
    patches, padded, centred, inv_std, normed, hidden, activated, projected = stored
    tile_total = padded.shape[0]
    reach = KERNEL // 2
    grid_grad = grad_mixed.reshape(tile_total, TILE, TILE, WIDTH)
    grad_padded = jnp.pad(grid_grad, ((0, 0), (reach, reach), (reach, reach), (0, 0)))
    kernel = depth_weight.astype(jnp.float32)
    depth_rows = []
    inner = jnp.zeros_like(grid_grad)
    for row_tap in range(KERNEL):
        for col_tap in range(KERNEL):
            window = padded[:, row_tap : row_tap + TILE, col_tap : col_tap + TILE, :]
            depth_rows.append(jnp.sum(window * grid_grad, axis=(0, 1, 2)))
            row_start = KERNEL - 1 - row_tap
            col_start = KERNEL - 1 - col_tap
            inner = (
                inner
                + grad_padded[:, row_start : row_start + TILE, col_start : col_start + TILE, :]
                * kernel[row_tap * KERNEL + col_tap]
            )
    depth_term = jnp.stack(depth_rows)
    grad_stem = (grad_block + inner.reshape(-1, WIDTH)).astype(jnp.bfloat16)
    stem_term = lax.dot_general(
        patches, grad_stem, (((0,), (0,)), ((), ())), preferred_element_type=jnp.float32
    )
    return (depth_term, stem_term)


def on_device(
    pixels,
    tile_counts,
    text_gaps,
    stem_weight,
    depth_weight,
    norm_gain,
    up_weight,
    down_weight,
    layer_scale,
    embed_grad,
):
    n_enc = lax.axis_size("enc")
    n_dec = lax.axis_size("dec")
    dec_here = lax.axis_index("dec")
    count_here = tile_counts[0, 0]
    block_rows = SLOTS * FEAT_TILE
    seq_rows = embed_grad.shape[1]
    weights = (stem_weight, depth_weight, norm_gain, up_weight, down_weight, layer_scale)
    column = lax.all_gather(
        jnp.concatenate([tile_counts[0], text_gaps[0]])[None, :], "dec", axis=0, tiled=True
    )
    col_counts = column[:, 0]
    col_gaps = column[:, 1]
    owner_span = col_counts * FEAT_TILE + col_gaps
    offsets = jnp.cumsum(owner_span) - owner_span + col_gaps
    dec_ids = jnp.arange(n_dec)
    own_offset = jnp.sum(jnp.where(dec_ids == dec_here, offsets, 0))
    occupied = jnp.arange(SLOTS) < count_here
    pooled, stored = encode(pixels[0], *weights)
    owner_block = (
        jnp.where(occupied[:, None, None], pooled, 0.0).astype(jnp.bfloat16).reshape(SLOTS, -1)
    )
    row_block = owner_block.reshape(block_rows, WIDTH)
    shard_rows = lax.all_gather(row_block, "dec", axis=0, tiled=True)
    row_total = shard_rows.shape[0]
    global_row = jnp.arange(row_total)
    source = global_row // block_rows
    within = global_row % block_rows
    pick_mask = dec_ids[None, :] == source[:, None]
    source_count = jnp.sum(jnp.where(pick_mask, col_counts[None, :], 0), axis=1)
    source_offset = jnp.sum(jnp.where(pick_mask, offsets[None, :], 0), axis=1)
    target = source_offset + within - dec_here * seq_rows
    keep_mask = (within < source_count * FEAT_TILE) & (target >= 0) & (target < seq_rows)
    target_row = jnp.where(keep_mask, target, seq_rows)
    sequence = (
        jnp.zeros((seq_rows, WIDTH), jnp.bfloat16).at[target_row].add(shard_rows, mode="drop")
    )
    shard_rows = lax.all_gather(embed_grad[0], "dec", axis=0, tiled=True)
    row_total = shard_rows.shape[0]
    row_ids = jnp.arange(block_rows)
    local_row = own_offset + row_ids
    inside = (local_row >= 0) & (local_row < row_total) & (row_ids < count_here * FEAT_TILE)
    taken_rows = jnp.take(shard_rows, jnp.clip(local_row, 0, row_total - 1), axis=0)
    own_grad = jnp.where(inside[:, None], taken_rows, jnp.zeros((block_rows, WIDTH), jnp.bfloat16))
    cotangent = own_grad.reshape(SLOTS, FEAT_TILE, WIDTH).astype(jnp.float32)
    scale_term, down_term, grad_hidden, grad_block = backward_head(
        stored, cotangent, down_weight, layer_scale
    )
    gain_term, up_term, grad_mixed = backward_middle(stored, grad_hidden, up_weight, norm_gain)
    depth_term, stem_term = backward_tail(stored, grad_mixed, grad_block, depth_weight)
    stem_sum, depth_sum, gain_sum, up_sum, down_sum, scale_sum = lax.psum(
        (stem_term, depth_term, gain_term, up_term, down_term, scale_term), ("enc", "dec")
    )
    grad_scale = 1.0 / math.sqrt(n_dec * n_enc * MEAN_TILES * FEAT_TILE)
    return (
        sequence[None],
        stem_sum * grad_scale,
        depth_sum * grad_scale,
        gain_sum * grad_scale,
        up_sum * grad_scale,
        down_sum * grad_scale,
        scale_sum * grad_scale,
    )


def solution(mesh):
    return jax.shard_map(
        on_device,
        mesh=mesh,
        in_specs=(
            P("dec", "enc", None),
            P("dec", "enc"),
            P("dec", "enc"),
            P(),
            P(),
            P(),
            P(),
            P(),
            P(),
            P("enc", "dec", None),
        ),
        out_specs=(P("enc", "dec", None), P(), P(), P(), P(), P(), P()),
        check_vma=False,
    )
```

profile of v0, /device:TPU:0, one launch (start us, length us, event | category | flops | bytes accessed | tf_op | source)
XLA Modules:
  0.0 234.0 jit_solution(1765711359585845056)
XLA Ops:
  7.2 0.8 convert_element_type.59
  8.1 0.7 slice_reduce_fusion.47
  8.8 0.7 slice_reduce_fusion.48
  10.8 1.2 dynamic-slice
  12.9 1.9 all-reduce.2
  15.3 1.2 fusion.117
  17.2 0.7 fusion.113
  17.9 1.7 reshape_squeeze.3
  19.6 2.2 all-gather.1
  21.8 0.9 gather_fusion
  23.8 1.2 fusion.7
  25.0 6.7 %fusion.119 = (f32[9,8,8]{2,1,0:T(8,128)S(1)}, f32[9,8,8,384]{3,2,1,0:T(8,128)S(1)}) fusion(f32[384]{0:T(512)} %get-tuple-element.59, f32[384]{0:T(512)} %get-tuple-element.60, f32[384]{0:T(512)} %get-tuple-element.61, f32[384]{0:T(512)} %get-tuple-element.62, f32[384]{0:T(512)} %get-tuple-element.63, f32[384]{0:T(512)} %get-tuple-element.64, ...), kind=kLoop, calls=%fused_computation.368 | loop fusion | flops 21675456 | bytes 1847040 | tf_op jit(solution)/shard_map/reduce_sum | solution.py:40
  31.7 0.7 div.36
  32.8 1.0 fusion.104
  34.6 1.4 fusion.6
  36.0 1.2 multiply_reduce_fusion.1
  37.2 1.7 fusion.105
  38.9 2.0 fusion.107
  40.9 1.6 multiply_reduce_fusion
  42.5 1.4 multiply_reduce_fusion.39
  44.3 2.6 %multiply_reduce_fusion.20 = (f32[384]{0:T(512)}, f32[384]{0:T(512)}, f32[384]{0:T(512)}, f32[384]{0:T(512)}, f32[384]{0:T(512)}, /*index=5*/f32[384]{0:T(512)},...) fusion(f32[9,8,8,384]{3,2,1,0:T(8,128)S(1)} %bitcast.36, ...), kind=kLoop, calls=%fused_computation.229 | loop fusion | flops 7955712 | bytes 1797120 | tf_op jit(solution)/shard_map/reduce_sum | solution.py:107
  46.9 2.2 multiply_reduce_fusion.2
  49.5 5.0 %fusion.96 = f32[9,8,8,384]{3,2,1,0:T(8,128)S(1)} fusion(f32[9,8,8,384]{3,2,1,0:T(8,128)S(1)} %bitcast.38, f32[384]{0:T(512)S(1)} %copy-done.27, f32[384]{0:T(512)S(1)} %copy-done.28, f32[384]{0:T(512)S(1)} %copy-done.29, f32[384]{0:T(512)S(1)} %copy-done.30, f32[384]{0:T(512)S(1)} %copy-done.31, f32[384]{0:T(512)S(1)} %copy-done.32, f32[384]{0:T(512)S(1)} %copy-done.33, ...), kind=kLoop, calls=%fused_computation.199 | loop fusion | flops 21454848 | bytes 1844736 | tf_op jit(solution)/shard_map/add | solution.py:111
  63.2 1.8 convolution_bitcast_fusion
  65.0 0.7 stack.198
  65.7 0.7 stack.180
  66.4 0.7 stack.179
  67.1 0.7 stack.178
  67.7 0.7 stack.177
  68.4 0.7 stack.176
  69.0 0.7 stack.175
  69.7 0.7 stack.173
  70.4 0.7 stack.172
  71.1 0.7 stack.171
  71.7 0.7 stack.170
  72.4 0.7 stack.169
  73.1 0.7 stack.168
  73.8 0.7 stack.167
  74.8 6.4 %stack.199 = f32[49,384]{1,0:T(8,128)} concatenate(f32[1,384]{1,0:T(1,128)} %stack.150, f32[1,384]{1,0:T(1,128)} %stack.151, f32[1,384]{1,0:T(1,128)} %stack.152, f32[1,384]{1,0:T(1,128)} %stack.153, f32[1,384]{1,0:T(1,128)} %stack.154, f32[1,384]{1,0:T(1,128)} %stack.155, f32[1,384]{1,0:T(1,128)} %stack.156, f32[1,384]{1,0:T(1,128)} %stack.157, f32[1,384]{1,0:T(1,128)} %stack.158, ...), dimensions={0} | concatenate | bytes 150528 | tf_op jit(solution)/shard_map/stack | solution.py:115
  81.8 0.8 reduce_sum.538
  83.1 2.0 all_gather.10
  85.1 3.0 %scatter_custom_fusion = bf16[208,384]{1,0:T(8,128)(2,1)} fusion(s32[288]{0:T(512)S(1)} %fusion.116, bf16[288,384]{1,0:T(8,128)(2,1)S(1)} %all_gather.10, bf16[]{:T(256)} %constant.33.clone.1), kind=kCustom, calls=%fused_computation.278 | custom fusion | flops 110592 | bytes 159746 | tf_op jit(solution)/shard_map/scatter-add | solution.py:169
  88.0 42.0 %all-reduce.3 = (f32[384]{0:T(512)S(1)}, f32[384]{0:T(512)S(1)}) all-reduce(f32[384]{0:T(512)S(1)} %copy-done.56, f32[384]{0:T(512)S(1)} %copy-done.57), channel_id=1, replica_groups=mesh['enc'=16,'dec'=2] {'enc','dec'}, use_global_device_ids=true, to_apply=%region_62.63 | all-reduce | flops 768 | bytes 6144 | tf_op jit(solution)/shard_map/psum | solution.py:184
  131.2 89.3 %all-reduce.7.cloned.1.call-done = (f32[48,384]{1,0:T(8,128)}, f32[49,384]{1,0:T(8,128)}, f32[384,768]{1,0:T(8,128)}, f32[768,384]{1,0:T(8,128)}) async-done(((f32[48,384]{1,0:T(8,128)}, f32[49,384]{1,0:T(8,128)}, f32[384,768]{1,0:T(8,128)}, f32[768,384]{1,0:T(8,128)}), (f32[48,384]{1,0:T(8,128)}, f32[49,384]{1,0:T(8,128)}, f32[384,768]{1,0:T(8,128)}, f32[768,384]{1,0:T(8,128)})) %all-reduce.7.cloned.1.call-update) | async-done | bytes 2508304 | tf_op jit(solution)/shard_map/psum | solution.py:184
  220.5 1.6 broadcast_multiply_fusion.4
  222.1 1.5 broadcast_multiply_fusion.3
  223.6 2.4 %broadcast_multiply_fusion.1 = f32[384,768]{1,0:T(8,128)} fusion(f32[384,768]{1,0:T(8,128)} %get-tuple-element.115), kind=kLoop, calls=%fused_computation.270 | loop fusion | flops 294912 | bytes 2359296 | tf_op jit(solution)/shard_map/mul | solution.py:193
  226.0 1.1 broadcast_multiply_fusion
  (197 shorter events, 14.7 us)
Async XLA Ops:
  7.2 27.4 %copy-start = (bf16[768,384]{1,0:T(8,128)(2,1)S(1)}, bf16[768,384]{1,0:T(8,128)(2,1)}, u32[]{:S(2)}) copy-start(bf16[768,384]{1,0:T(8,128)(2,1)} %param.17) | copy-start | bytes 1769476
  7.2 213.3 %all-reduce.7.cloned.1.call-start = ((), (), s32[]{:S(2)}) async-start(), calls=%async_computation | async-start | bytes 5038080 | tf_op jit(solution)/shard_map/psum | solution.py:184
  8.8 16.2 %copy-start.5 = (f32[384]{0:T(512)}, f32[384]{0:T(512)S(1)}, u32[]{:S(2)}) copy-start(f32[384]{0:T(512)S(1)} %get-tuple-element.77) | copy-start | bytes 4612
  8.8 16.2 %copy-start.7 = (f32[384]{0:T(512)}, f32[384]{0:T(512)S(1)}, u32[]{:S(2)}) copy-start(f32[384]{0:T(512)S(1)} %get-tuple-element.78) | copy-start | bytes 4612
  43.9 5.2 %copy-start.6 = (f32[384]{0:T(512)S(1)}, f32[384]{0:T(512)}, u32[]{:S(2)}) copy-start(f32[384]{0:T(512)} %copy-done.5) | copy-start | bytes 4612
  43.9 5.2 %copy-start.8 = (f32[384]{0:T(512)S(1)}, f32[384]{0:T(512)}, u32[]{:S(2)}) copy-start(f32[384]{0:T(512)} %copy-done.7) | copy-start | bytes 4612
  43.9 5.2 %copy-start.9 = (f32[384]{0:T(512)S(1)}, f32[384]{0:T(512)}, u32[]{:S(2)}) copy-start(f32[384]{0:T(512)} %get-tuple-element.79) | copy-start | bytes 4612
  44.0 5.2 %copy-start.10 = (f32[384]{0:T(512)S(1)}, f32[384]{0:T(512)}, u32[]{:S(2)}) copy-start(f32[384]{0:T(512)} %get-tuple-element.80) | copy-start | bytes 4612
  44.0 5.2 %copy-start.11 = (f32[384]{0:T(512)S(1)}, f32[384]{0:T(512)}, u32[]{:S(2)}) copy-start(f32[384]{0:T(512)} %get-tuple-element.81) | copy-start | bytes 4612
  44.0 5.2 %copy-start.12 = (f32[384]{0:T(512)S(1)}, f32[384]{0:T(512)}, u32[]{:S(2)}) copy-start(f32[384]{0:T(512)} %get-tuple-element.82) | copy-start | bytes 4612
  44.0 5.2 %copy-start.13 = (f32[384]{0:T(512)S(1)}, f32[384]{0:T(512)}, u32[]{:S(2)}) copy-start(f32[384]{0:T(512)} %get-tuple-element.83) | copy-start | bytes 4612
  44.0 5.2 %copy-start.14 = (f32[384]{0:T(512)S(1)}, f32[384]{0:T(512)}, u32[]{:S(2)}) copy-start(f32[384]{0:T(512)} %get-tuple-element.84) | copy-start | bytes 4612
  44.0 5.2 %copy-start.15 = (f32[384]{0:T(512)S(1)}, f32[384]{0:T(512)}, u32[]{:S(2)}) copy-start(f32[384]{0:T(512)} %get-tuple-element.85) | copy-start | bytes 4612
  44.0 5.2 %copy-start.16 = (f32[384]{0:T(512)S(1)}, f32[384]{0:T(512)}, u32[]{:S(2)}) copy-start(f32[384]{0:T(512)} %get-tuple-element.86) | copy-start | bytes 4612
  44.0 5.2 %copy-start.17 = (f32[384]{0:T(512)S(1)}, f32[384]{0:T(512)}, u32[]{:S(2)}) copy-start(f32[384]{0:T(512)} %get-tuple-element.87) | copy-start | bytes 4612
  44.0 5.2 %copy-start.18 = (f32[384]{0:T(512)S(1)}, f32[384]{0:T(512)}, u32[]{:S(2)}) copy-start(f32[384]{0:T(512)} %get-tuple-element.88) | copy-start | bytes 4612
  44.0 5.2 %copy-start.19 = (f32[384]{0:T(512)S(1)}, f32[384]{0:T(512)}, u32[]{:S(2)}) copy-start(f32[384]{0:T(512)} %get-tuple-element.89) | copy-start | bytes 4612
  44.1 5.2 %copy-start.20 = (f32[384]{0:T(512)S(1)}, f32[384]{0:T(512)}, u32[]{:S(2)}) copy-start(f32[384]{0:T(512)} %get-tuple-element.90) | copy-start | bytes 4612
  44.1 5.2 %copy-start.21 = (f32[384]{0:T(512)S(1)}, f32[384]{0:T(512)}, u32[]{:S(2)}) copy-start(f32[384]{0:T(512)} %get-tuple-element.91) | copy-start | bytes 4612
  44.1 5.2 %copy-start.22 = (f32[384]{0:T(512)S(1)}, f32[384]{0:T(512)}, u32[]{:S(2)}) copy-start(f32[384]{0:T(512)} %get-tuple-element.92) | copy-start | bytes 4612
  44.1 5.2 %copy-start.23 = (f32[384]{0:T(512)S(1)}, f32[384]{0:T(512)}, u32[]{:S(2)}) copy-start(f32[384]{0:T(512)} %get-tuple-element.93) | copy-start | bytes 4612
  44.1 5.2 %copy-start.24 = (f32[384]{0:T(512)S(1)}, f32[384]{0:T(512)}, u32[]{:S(2)}) copy-start(f32[384]{0:T(512)} %get-tuple-element.94) | copy-start | bytes 4612
  44.1 5.2 %copy-start.25 = (f32[384]{0:T(512)S(1)}, f32[384]{0:T(512)}, u32[]{:S(2)}) copy-start(f32[384]{0:T(512)} %get-tuple-element.95) | copy-start | bytes 4612
  44.1 5.2 %copy-start.26 = (f32[384]{0:T(512)S(1)}, f32[384]{0:T(512)}, u32[]{:S(2)}) copy-start(f32[384]{0:T(512)} %get-tuple-element.58) | copy-start | bytes 4612
  44.1 5.2 %copy-start.27 = (f32[384]{0:T(512)S(1)}, f32[384]{0:T(512)}, u32[]{:S(2)}) copy-start(f32[384]{0:T(512)} %get-tuple-element.59) | copy-start | bytes 4612
  44.1 5.2 %copy-start.28 = (f32[384]{0:T(512)S(1)}, f32[384]{0:T(512)}, u32[]{:S(2)}) copy-start(f32[384]{0:T(512)} %get-tuple-element.60) | copy-start | bytes 4612
  44.1 5.2 %copy-start.29 = (f32[384]{0:T(512)S(1)}, f32[384]{0:T(512)}, u32[]{:S(2)}) copy-start(f32[384]{0:T(512)} %get-tuple-element.61) | copy-start | bytes 4612
  44.2 5.2 %copy-start.30 = (f32[384]{0:T(512)S(1)}, f32[384]{0:T(512)}, u32[]{:S(2)}) copy-start(f32[384]{0:T(512)} %get-tuple-element.62) | copy-start | bytes 4612
  44.2 5.2 %copy-start.31 = (f32[384]{0:T(512)S(1)}, f32[384]{0:T(512)}, u32[]{:S(2)}) copy-start(f32[384]{0:T(512)} %get-tuple-element.63) | copy-start | bytes 4612
  44.2 5.2 %copy-start.32 = (f32[384]{0:T(512)S(1)}, f32[384]{0:T(512)}, u32[]{:S(2)}) copy-start(f32[384]{0:T(512)} %get-tuple-element.64) | copy-start | bytes 4612
  44.2 5.2 %copy-start.33 = (f32[384]{0:T(512)S(1)}, f32[384]{0:T(512)}, u32[]{:S(2)}) copy-start(f32[384]{0:T(512)} %get-tuple-element.65) | copy-start | bytes 4612
  44.2 5.2 %copy-start.34 = (f32[384]{0:T(512)S(1)}, f32[384]{0:T(512)}, u32[]{:S(2)}) copy-start(f32[384]{0:T(512)} %get-tuple-element.66) | copy-start | bytes 4612
  44.2 5.2 %copy-start.35 = (f32[384]{0:T(512)S(1)}, f32[384]{0:T(512)}, u32[]{:S(2)}) copy-start(f32[384]{0:T(512)} %get-tuple-element.67) | copy-start | bytes 4612
  44.2 5.2 %copy-start.36 = (f32[384]{0:T(512)S(1)}, f32[384]{0:T(512)}, u32[]{:S(2)}) copy-start(f32[384]{0:T(512)} %get-tuple-element.68) | copy-start | bytes 4612
  62.5 11.9 %copy-start.55 = (f32[384]{0:T(512)S(1)}, f32[384]{0:T(512)}, u32[]{:S(2)}) copy-start(f32[384]{0:T(512)} %get-tuple-element.40) | copy-start | bytes 4612
  62.5 11.9 %copy-start.54 = (f32[384]{0:T(512)S(1)}, f32[384]{0:T(512)}, u32[]{:S(2)}) copy-start(f32[384]{0:T(512)} %get-tuple-element.41) | copy-start | bytes 4612
  62.5 11.9 %copy-start.53 = (f32[384]{0:T(512)S(1)}, f32[384]{0:T(512)}, u32[]{:S(2)}) copy-start(f32[384]{0:T(512)} %get-tuple-element.42) | copy-start | bytes 4612
  62.5 11.9 %copy-start.52 = (f32[384]{0:T(512)S(1)}, f32[384]{0:T(512)}, u32[]{:S(2)}) copy-start(f32[384]{0:T(512)} %get-tuple-element.43) | copy-start | bytes 4612
  62.6 11.9 %copy-start.50 = (f32[384]{0:T(512)S(1)}, f32[384]{0:T(512)}, u32[]{:S(2)}) copy-start(f32[384]{0:T(512)} %get-tuple-element.44) | copy-start | bytes 4612
  62.6 11.9 %copy-start.51 = (f32[384]{0:T(512)S(1)}, f32[384]{0:T(512)}, u32[]{:S(2)}) copy-start(f32[384]{0:T(512)} %get-tuple-element.10) | copy-start | bytes 4612
  62.6 11.9 %copy-start.49 = (f32[384]{0:T(512)S(1)}, f32[384]{0:T(512)}, u32[]{:S(2)}) copy-start(f32[384]{0:T(512)} %get-tuple-element.11) | copy-start | bytes 4612
  62.6 12.0 %copy-start.48 = (f32[384]{0:T(512)S(1)}, f32[384]{0:T(512)}, u32[]{:S(2)}) copy-start(f32[384]{0:T(512)} %get-tuple-element.12) | copy-start | bytes 4612
  62.6 12.0 %copy-start.47 = (f32[384]{0:T(512)S(1)}, f32[384]{0:T(512)}, u32[]{:S(2)}) copy-start(f32[384]{0:T(512)} %get-tuple-element.13) | copy-start | bytes 4612
  62.6 12.0 %copy-start.46 = (f32[384]{0:T(512)S(1)}, f32[384]{0:T(512)}, u32[]{:S(2)}) copy-start(f32[384]{0:T(512)} %get-tuple-element.14) | copy-start | bytes 4612
  62.6 12.0 %copy-start.45 = (f32[384]{0:T(512)S(1)}, f32[384]{0:T(512)}, u32[]{:S(2)}) copy-start(f32[384]{0:T(512)} %get-tuple-element.15) | copy-start | bytes 4612
  81.2 6.8 %copy-start.56 = (f32[384]{0:T(512)S(1)}, f32[384]{0:T(512)}, u32[]{:S(2)}) copy-start(f32[384]{0:T(512)} %get-tuple-element.7) | copy-start | bytes 4612
  81.3 6.8 %copy-start.57 = (f32[384]{0:T(512)S(1)}, f32[384]{0:T(512)}, u32[]{:S(2)}) copy-start(f32[384]{0:T(512)} %get-tuple-element.123) | copy-start | bytes 4612
  220.5 5.5 %copy-start.2 = (f32[768,384]{1,0:T(8,128)S(1)}, f32[768,384]{1,0:T(8,128)}, u32[]{:S(2)}) copy-start(f32[768,384]{1,0:T(8,128)} %get-tuple-element.116) | copy-start | bytes 3538948
  (15 other events, 52.7 us)
Sparse Core Ops, SparseCore 0:
  81.3 139.1 all-reduce.6
where the time goes:
time: 235 us; the launch traced here: 234 us
  waiting for transfers between devices  89.3 us (38%)
  blocking collectives  48.1 us (20%)
  other arithmetic  35.5 us (15%)
  local copies, waits for them, and re-layouts  32.3 us (14%)
  between operations  17.3 us (7%)
  matrix products  11.5 us (5%)
    psum x1, waiting for transfers between devices, on_device(): lax.psum((stem_term, depth_term, gain_term, up_term, down_term, scale_ter...  89.3 us
    psum x1, blocking collectives, on_device(): lax.psum((stem_term, depth_term, gain_term, up_term, down_term, scale_ter...  42 us
    another operation x50, local copies, waits for them, and re-layouts, backward_tail(): depth_term = jnp.stack(depth_rows)  23.4 us
    reduce_sum x1, other arithmetic, encode(): channel_mean = jnp.mean(flat_rows, axis=1, keepdims=True)  6.67 us
    reduce_sum x3, other arithmetic, backward_tail(): depth_rows.append(jnp.sum(window * grid_grad, axis=(0, 1, 2)))  6.26 us
    add x1, other arithmetic, backward_tail(): inner + grad_padded[:, row_start:row_start + TILE, col_start:col_start +...  4.97 us
  transfers between devices with their start and end apart: 1, of which 1 were waited for; matrix products, arithmetic and copies ran while one was open for 3% of the time, Pallas kernels for 0%

commit v1 on v0

v1 whole, which is shorter than its diff:
```python
import functools
import math

import jax
import jax.numpy as jnp
from jax import lax
from jax.experimental import pallas as pl
from jax.experimental.pallas import tpu as pltpu
from jax.sharding import PartitionSpec as P

WIDTH = 384
INNER = 768
KERNEL = 7
REACH = 3
PATCH_CH = 48
TILE = 8
MEAN_TILES = 3
FEAT_TILE = 16
LANES = 128
GROUPS = WIDTH // LANES
EPSILON = 1e-06
GELU_A = math.sqrt(2.0 / math.pi)
GELU_B = 0.044715
MESH = pl.DeviceIdType.MESH

UP_AT = 0
DOWN_AT = UP_AT + (INNER // LANES) * WIDTH
STEM_AT = DOWN_AT + GROUPS * INNER
SMALL_AT = STEM_AT + GROUPS * PATCH_CH
SMALL = 64
PACKED = SMALL_AT + GROUPS * SMALL
GAIN_ROW = 56
SCALE_ROW = 57

NT = (((1,), (1,)), ((), ()))
TN = (((0,), (0,)), ((), ()))


def dot(left, right, dims=(((1,), (0,)), ((), ()))):
    return lax.dot_general(left, right, dims, preferred_element_type=jnp.float32)


def vmem():
    return pl.BlockSpec(memory_space=pltpu.VMEM)


def gather_kernel(n_dec, grad_ref, count_ref, gap_ref, full_ref, meta_ref, info, sends, recvs):
    enc_here = lax.axis_index("enc")
    dec_here = lax.axis_index("dec")
    seq_rows = grad_ref.shape[1]
    count = count_ref[0, 0]
    gap = gap_ref[0, 0]
    barrier = pltpu.get_barrier_semaphore()
    for step in range(1, n_dec):
        peer = lax.rem(dec_here + step, n_dec)
        pl.semaphore_signal(barrier, inc=1, device_id=(enc_here, peer), device_id_type=MESH)
    mine = pl.ds(pl.multiple_of(dec_here * 16, 16), 16)
    info[mine, :] = jnp.concatenate(
        [jnp.full((8, LANES), count, jnp.int32), jnp.full((8, LANES), gap, jnp.int32)], axis=0
    )
    pl.semaphore_wait(barrier, n_dec - 1)
    rows = pl.ds(pl.multiple_of(dec_here * seq_rows, 16), seq_rows)
    copies = []
    for step in range(1, n_dec):
        peer = lax.rem(dec_here + step, n_dec)
        for kind, (source, target) in enumerate(
            ((info.at[mine], info.at[mine]), (grad_ref.at[0], full_ref.at[rows]))
        ):
            copy = pltpu.make_async_remote_copy(
                src_ref=source,
                dst_ref=target,
                send_sem=sends.at[step - 1, kind],
                recv_sem=recvs.at[step - 1, kind],
                device_id=(enc_here, peer),
                device_id_type=MESH,
            )
            copy.start()
            copies.append(copy)
    full_ref[rows, :] = grad_ref[0]
    for copy in copies:
        copy.wait()
    start = jnp.full((8, LANES), gap, jnp.int32)
    for other in range(n_dec):
        span = info[other * 16 : other * 16 + 8, :] * FEAT_TILE + info[
            other * 16 + 8 : other * 16 + 16, :
        ]
        start = start + jnp.where(other < dec_here, span, 0)
    meta_ref[0:8, :] = start
    meta_ref[8:16, :] = jnp.full((8, LANES), count, jnp.int32)


def gather(n_dec, grad, counts, gaps):
    seq_rows = grad.shape[1]
    steps = max(n_dec - 1, 1)
    return pl.pallas_call(
        functools.partial(gather_kernel, n_dec),
        out_shape=(
            jax.ShapeDtypeStruct((n_dec * seq_rows, WIDTH), jnp.bfloat16),
            jax.ShapeDtypeStruct((16, LANES), jnp.int32),
        ),
        in_specs=[
            vmem(),
            pl.BlockSpec(memory_space=pltpu.SMEM),
            pl.BlockSpec(memory_space=pltpu.SMEM),
        ],
        out_specs=(vmem(), vmem()),
        scratch_shapes=[
            pltpu.VMEM((n_dec * 16, LANES), jnp.int32),
            pltpu.SemaphoreType.DMA((steps, 2)),
            pltpu.SemaphoreType.DMA((steps, 2)),
        ],
        compiler_params=pltpu.CompilerParams(collective_id=0, has_side_effects=True),
        name="gather_dec",
    )(grad, counts, gaps)


def shift_rows(value, amount):
    if amount == 0:
        return value
    row = lax.broadcasted_iota(jnp.int32, value.shape, 0)
    inside = (row + amount >= 0) & (row + amount < TILE)
    return jnp.where(inside, pltpu.roll(value, (-amount) % TILE, 0), 0.0)


def tower_kernel(
    tiles,
    pixels_ref,
    meta_ref,
    grad_ref,
    stem_ref,
    depth_ref,
    gain_ref,
    up_ref,
    down_ref,
    layer_ref,
    place_ref,
    pack_ref,
    wide,
    rows_in,
    stem_out,
    field,
    taps,
    normed_all,
    act_all,
    proj_all,
    hid_all,
    block_all,
    pool,
    depth_acc,
    small_acc,
):
    span = tiles * TILE
    chunk = 2 * span
    seq = grad_ref.shape[0]
    start = meta_ref[0:1, 0:1]
    count = meta_ref[8:9, 0:1]

    wide[...] = jnp.zeros_like(wide)
    for col in range(TILE):
        wide[col * PATCH_CH : (col + 1) * PATCH_CH, col * WIDTH : (col + 1) * WIDTH] = stem_ref[...]
    for tap in range(KERNEL * KERNEL):
        taps[tap * 8 : tap * 8 + 8, :] = jnp.broadcast_to(
            depth_ref[tap : tap + 1, :].astype(jnp.float32), (8, WIDTH)
        )
    depth_acc[...] = jnp.zeros_like(depth_acc)
    small_acc[...] = jnp.zeros_like(small_acc)
    pix = pixels_ref[...].astype(jnp.float32)
    for tile in range(tiles):
        rows_in[tile * 8 : tile * 8 + 8, :] = jnp.concatenate(
            [pix[tile : tile + 1, r * WIDTH : (r + 1) * WIDTH] for r in range(TILE)], axis=0
        )
    rows = rows_in[...].astype(jnp.bfloat16)
    for col in range(TILE):
        stem_out[col * span : (col + 1) * span, :] = (
            dot(rows, wide[:, col * WIDTH : (col + 1) * WIDTH])
            .astype(jnp.bfloat16)
            .astype(jnp.float32)
        )

    def at(col, tile):
        return pl.ds(pl.multiple_of(col * span + tile * 8, 8), 8)

    def mix(tile, carry):
        for group in range(GROUPS):
            lanes = slice(group * LANES, (group + 1) * LANES)
            source = [stem_out[at(col, tile), lanes] for col in range(TILE)]
            total = [jnp.zeros((8, LANES), jnp.float32)] * TILE
            for a in range(KERNEL):
                moved = [shift_rows(value, a - REACH) for value in source]
                for b in range(KERNEL):
                    tap = a * KERNEL + b
                    weight = taps[tap * 8 : tap * 8 + 8, lanes]
                    for col in range(TILE):
                        other = col + b - REACH
                        if 0 <= other < TILE:
                            total[col] = total[col] + moved[other] * weight
            for col in range(TILE):
                field[at(col, tile), lanes] = total[col]
        return carry

    lax.fori_loop(0, tiles, mix, 0)

    gain = gain_ref[...]
    layer = layer_ref[...]

    def fold(value):
        return jnp.sum(value.reshape(-1, 8, WIDTH), axis=0)

    def block(pair, carry):
        here = pl.ds(pl.multiple_of(pair * chunk, 16), chunk)
        mixed = field[here, :]
        dev = mixed - jnp.mean(mixed, axis=1, keepdims=True)
        inv = lax.rsqrt(jnp.mean(dev * dev, axis=1, keepdims=True) + EPSILON)
        centred = dev * inv
        normed = (centred * gain).astype(jnp.bfloat16)
        normed_all[here, :] = normed
        hidden = dot(normed, up_ref[...])
        square = hidden * hidden
        half = 0.5 + 0.5 * jnp.tanh(GELU_A * hidden * (1.0 + GELU_B * square))
        act = (hidden * half).astype(jnp.bfloat16)
        slope = half + hidden * (2.0 * half * (1.0 - half)) * (
            GELU_A + (3.0 * GELU_A * GELU_B) * square
        )
        act_all[here, :] = act
        projected = dot(act, down_ref[...])
        out = stem_out[here, :] + layer * projected
        both = out[:span] + out[span:]
        both = both + pltpu.roll(both, span - 1, 0)
        pool[pl.ds(pl.multiple_of(pair * span, 8), span), :] = 0.25 * both

        row = lax.broadcasted_iota(jnp.int32, (span, seq), 0)
        spot = lax.broadcasted_iota(jnp.int32, (span, seq), 1)
        tile = row // TILE
        want = start + tile * FEAT_TILE + (row % TILE) // 2 * 4 + pair
        pick = jnp.where((spot == want) & (tile < count), 0.25, 0.0).astype(jnp.bfloat16)
        once = dot(pick, grad_ref[...])
        grad_block = jnp.concatenate([once, once], axis=0)
        block_all[here, :] = grad_block
        small_acc[0:8, :] += fold(grad_block * projected)
        grad_proj = (grad_block * layer).astype(jnp.bfloat16)
        proj_all[here, :] = grad_proj
        grad_act = dot(grad_proj, down_ref[...], NT)
        grad_hidden = (grad_act * slope).astype(jnp.bfloat16)
        hid_all[here, :] = grad_hidden
        grad_normed = dot(grad_hidden, up_ref[...], NT)
        small_acc[8:16, :] += fold(grad_normed * centred)
        scaled = grad_normed * gain
        field[here, :] = inv * (
            scaled
            - jnp.mean(scaled, axis=1, keepdims=True)
            - centred * jnp.mean(scaled * centred, axis=1, keepdims=True)
        )
        return carry

    lax.fori_loop(0, TILE // 2, block, 0)

    place = jnp.zeros((seq, WIDTH), jnp.float32)
    for pair in range(TILE // 2):
        spot = lax.broadcasted_iota(jnp.int32, (seq, span), 0)
        row = lax.broadcasted_iota(jnp.int32, (seq, span), 1)
        tile = row // TILE
        want = start + tile * FEAT_TILE + (row % TILE) // 2 * 4 + pair
        hit = (spot == want) & (tile < count) & (row % 2 == 0)
        place = place + dot(
            jnp.where(hit, 1.0, 0.0).astype(jnp.bfloat16),
            pool[pair * span : (pair + 1) * span, :].astype(jnp.bfloat16),
        )
    place_ref[...] = place.astype(jnp.bfloat16)

    def pack(first, value):
        height = value.shape[0]
        for group in range(value.shape[1] // LANES):
            at_row = first + group * height
            pack_ref[at_row : at_row + height, :] = value[
                :, group * LANES : (group + 1) * LANES
            ].astype(jnp.bfloat16)

    pack(UP_AT, dot(normed_all[...], hid_all[...], TN))
    pack(DOWN_AT, dot(act_all[...], proj_all[...], TN))

    def unmix(tile, carry):
        for group in range(GROUPS):
            lanes = slice(group * LANES, (group + 1) * LANES)
            grads = [field[at(col, tile), lanes] for col in range(TILE)]
            source = [stem_out[at(col, tile), lanes] for col in range(TILE)]
            total = [block_all[at(col, tile), lanes] for col in range(TILE)]
            for a in range(KERNEL):
                moved = [shift_rows(value, REACH - a) for value in grads]
                for b in range(KERNEL):
                    tap = a * KERNEL + b
                    weight = taps[tap * 8 : tap * 8 + 8, lanes]
                    term = None
                    for col in range(TILE):
                        other = col - b + REACH
                        if 0 <= other < TILE:
                            total[col] = total[col] + moved[other] * weight
                            product = moved[other] * source[col]
                            term = product if term is None else term + product
                    depth_acc[tap * 8 : tap * 8 + 8, lanes] += term
            for col in range(TILE):
                block_all[at(col, tile), lanes] = total[col]
        return carry

    lax.fori_loop(0, tiles, unmix, 0)

    stem_term = jnp.zeros((PATCH_CH, WIDTH), jnp.float32)
    for col in range(TILE):
        grad_stem = block_all[col * span : (col + 1) * span, :].astype(jnp.bfloat16)
        stem_term = (
            stem_term + dot(rows, grad_stem, TN)[col * PATCH_CH : (col + 1) * PATCH_CH, :]
        )
    pack(STEM_AT, stem_term)
    taps_sum = jnp.sum(depth_acc[...].reshape(KERNEL * KERNEL, 8, WIDTH), axis=1)
    small = jnp.concatenate(
        [
            taps_sum,
            jnp.zeros((GAIN_ROW - KERNEL * KERNEL, WIDTH), jnp.float32),
            jnp.sum(small_acc[8:16, :], axis=0, keepdims=True),
            jnp.sum(small_acc[0:8, :], axis=0, keepdims=True),
            jnp.zeros((SMALL - SCALE_ROW - 1, WIDTH), jnp.float32),
        ],
        axis=0,
    )
    pack(SMALL_AT, small)
    if pack_ref.shape[0] > PACKED:
        pack_ref[PACKED:, :] = jnp.zeros((pack_ref.shape[0] - PACKED, LANES), jnp.bfloat16)


def tower(packed_rows, pixels, meta, grad, weights):
    tiles = pixels.shape[0]
    positions = tiles * TILE * TILE
    span = tiles * TILE
    stem_weight, depth_weight, norm_gain, up_weight, down_weight, layer_scale = weights
    f32, bf16 = jnp.float32, jnp.bfloat16
    return pl.pallas_call(
        functools.partial(tower_kernel, tiles),
        out_shape=(
            jax.ShapeDtypeStruct(grad.shape, bf16),
            jax.ShapeDtypeStruct((packed_rows, LANES), bf16),
        ),
        in_specs=[vmem()] * 9,
        out_specs=(vmem(), vmem()),
        scratch_shapes=[
            pltpu.VMEM((WIDTH, TILE * WIDTH), bf16),
            pltpu.VMEM((span, WIDTH), f32),
            pltpu.VMEM((positions, WIDTH), f32),
            pltpu.VMEM((positions, WIDTH), f32),
            pltpu.VMEM((KERNEL * KERNEL * 8, WIDTH), f32),
            pltpu.VMEM((positions, WIDTH), bf16),
            pltpu.VMEM((positions, INNER), bf16),
            pltpu.VMEM((positions, WIDTH), bf16),
            pltpu.VMEM((positions, INNER), bf16),
            pltpu.VMEM((positions, WIDTH), f32),
            pltpu.VMEM((positions // 2, WIDTH), f32),
            pltpu.VMEM((KERNEL * KERNEL * 8, WIDTH), f32),
            pltpu.VMEM((16, WIDTH), f32),
        ],
        compiler_params=pltpu.CompilerParams(vmem_limit_bytes=48 * 2**20),
        name="tower",
    )(
        pixels,
        meta,
        grad,
        stem_weight,
        depth_weight,
        norm_gain.reshape(1, WIDTH),
        up_weight,
        down_weight,
        layer_scale.reshape(1, WIDTH),
    )


def enc_factors(n_enc):
    if n_enc == 16:
        sizes = [2, 2, 4]
    else:
        sizes, left = [], n_enc
        while left > 1:
            size = next((s for s in (4, 2, 3, 5, 7) if left % s == 0), left)
            sizes.append(size)
            left //= size
    steps, stride = [], 1
    for size in sizes:
        steps.append((stride, size))
        stride *= size
    return steps


def reduce_kernel(n_enc, n_dec, scale, pack_ref, place_ref, *refs):
    factors = enc_factors(n_enc)
    sizes = [n_dec] + [size for _, size in factors]
    depth = len(sizes)
    seq_ref, stem_ref, depth_ref, gain_ref, up_ref, down_ref, scale_ref = refs[:7]
    held = refs[7 : 7 + depth]
    landed = refs[7 + depth : 7 + 2 * depth]
    full, place_in, place_send, place_recv, sum_send, sum_recv, out_send, out_recv = refs[
        7 + 2 * depth :
    ]
    enc_here = lax.axis_index("enc")
    dec_here = lax.axis_index("dec")
    odd = lax.rem(dec_here, 2)

    indices, peers = [dec_here], []
    peers.append([(enc_here, lax.rem(dec_here + s, n_dec)) for s in range(1, n_dec)])
    swap = len(factors) > 1 and factors[0][1] == factors[1][1]
    for place, (stride, size) in enumerate(factors):
        if swap and place < 2:
            other = factors[1 - place][0]
            stride = jnp.where(odd == 1, other, stride)
        index = lax.rem(lax.div(enc_here, stride), size)
        indices.append(index)
        peers.append(
            [
                (enc_here + (lax.rem(index + s, size) - index) * stride, dec_here)
                for s in range(1, size)
            ]
        )

    barrier = pltpu.get_barrier_semaphore()
    greeted = 0
    for group in peers:
        for peer in group:
            pl.semaphore_signal(barrier, inc=1, device_id=peer, device_id_type=MESH)
            greeted += 1
    pl.semaphore_wait(barrier, greeted)

    def send(source, target, send_sem, recv_sem, peer):
        copy = pltpu.make_async_remote_copy(
            src_ref=source,
            dst_ref=target,
            send_sem=send_sem,
            recv_sem=recv_sem,
            device_id=peer,
            device_id_type=MESH,
        )
        copy.start()
        return copy

    seq_rows = seq_ref.shape[1]
    waiting = []
    offset = 0
    offsets = []
    height = pack_ref.shape[0]
    sem = 0
    for stage in range(depth):
        size = sizes[stage]
        source = pack_ref if stage == 0 else held[stage - 1]
        part = height // size
        copies = []
        for step in range(1, size):
            index = lax.rem(indices[stage] + step, size)
            copies.append(
                send(
                    source.at[pl.ds(pl.multiple_of(index * part, 16), part)],
                    landed[stage].at[step - 1],
                    sum_send.at[sem],
                    sum_recv.at[sem],
                    peers[stage][step - 1],
                )
            )
            sem += 1
        if stage == 0:
            places = []
            for step in range(1, size):
                index = lax.rem(dec_here + step, size)
                places.append(
                    send(
                        place_ref.at[pl.ds(pl.multiple_of(index * seq_rows, 16), seq_rows)],
                        place_in.at[step - 1],
                        place_send.at[step - 1],
                        place_recv.at[step - 1],
                        peers[0][step - 1],
                    )
                )
        total = source[pl.ds(pl.multiple_of(indices[stage] * part, 16), part), :].astype(
            jnp.float32
        )
        for step, copy in enumerate(copies):
            copy.wait_recv()
            total = total + landed[stage][step].astype(jnp.float32)
        waiting += copies
        offset = offset + indices[stage] * part
        offsets.append(offset)
        height = part
        if stage < depth - 1:
            held[stage][...] = total.astype(jnp.bfloat16)
        else:
            full[pl.ds(pl.multiple_of(offset, 16), part), :] = total.astype(jnp.bfloat16)

    sem = 0
    for stage in reversed(range(depth)):
        mine = full.at[pl.ds(pl.multiple_of(offsets[stage], 16), height)]
        copies = []
        for step in range(1, sizes[stage]):
            copies.append(
                send(mine, mine, out_send.at[sem], out_recv.at[sem], peers[stage][step - 1])
            )
            sem += 1
        if stage == depth - 1:
            sequence = place_ref[
                pl.ds(pl.multiple_of(dec_here * seq_rows, 16), seq_rows), :
            ].astype(jnp.float32)
            for step, copy in enumerate(places):
                copy.wait_recv()
                sequence = sequence + place_in[step].astype(jnp.float32)
            seq_ref[0] = sequence.astype(jnp.bfloat16)
            waiting += places
        for copy in copies:
            copy.wait_recv()
        waiting += copies
        height *= sizes[stage]
    for copy in waiting:
        copy.wait_send()

    def unpack(first, rows, group):
        at_row = first + group * rows
        return full[at_row : at_row + rows, :].astype(jnp.float32) * scale

    for group in range(INNER // LANES):
        up_ref[:, group * LANES : (group + 1) * LANES] = unpack(UP_AT, WIDTH, group)
    for group in range(GROUPS):
        lanes = slice(group * LANES, (group + 1) * LANES)
        down_ref[:, lanes] = unpack(DOWN_AT, INNER, group)
        stem_ref[:, lanes] = unpack(STEM_AT, PATCH_CH, group)
        small = unpack(SMALL_AT, SMALL, group)
        depth_ref[:, lanes] = small[: KERNEL * KERNEL]
        gain_ref[:, lanes] = small[GAIN_ROW : GAIN_ROW + 1]
        scale_ref[:, lanes] = small[SCALE_ROW : SCALE_ROW + 1]


def reduce_all(n_enc, n_dec, scale, packed, place):
    sizes = [n_dec] + [size for _, size in enc_factors(n_enc)]
    rows = packed.shape[0]
    seq_rows = place.shape[0] // n_dec
    f32, bf16 = jnp.float32, jnp.bfloat16
    held, landed, height = [], [], rows
    for size in sizes:
        height //= size
        held.append(pltpu.VMEM((height, LANES), bf16))
        landed.append(pltpu.VMEM((max(size - 1, 1), height, LANES), bf16))
    steps = max(sum(size - 1 for size in sizes), 1)
    places = max(n_dec - 1, 1)
    return pl.pallas_call(
        functools.partial(reduce_kernel, n_enc, n_dec, scale),
        out_shape=(
            jax.ShapeDtypeStruct((1, seq_rows, WIDTH), bf16),
            jax.ShapeDtypeStruct((PATCH_CH, WIDTH), f32),
            jax.ShapeDtypeStruct((KERNEL * KERNEL, WIDTH), f32),
            jax.ShapeDtypeStruct((1, WIDTH), f32),
            jax.ShapeDtypeStruct((WIDTH, INNER), f32),
            jax.ShapeDtypeStruct((INNER, WIDTH), f32),
            jax.ShapeDtypeStruct((1, WIDTH), f32),
        ),
        in_specs=[vmem()] * 2,
        out_specs=(vmem(),) * 7,
        scratch_shapes=held
        + landed
        + [
            pltpu.VMEM((rows, LANES), bf16),
            pltpu.VMEM((places, seq_rows, WIDTH), bf16),
            pltpu.SemaphoreType.DMA((places,)),
            pltpu.SemaphoreType.DMA((places,)),
            pltpu.SemaphoreType.DMA((steps,)),
            pltpu.SemaphoreType.DMA((steps,)),
            pltpu.SemaphoreType.DMA((steps,)),
            pltpu.SemaphoreType.DMA((steps,)),
        ],
        compiler_params=pltpu.CompilerParams(
            collective_id=1, has_side_effects=True, vmem_limit_bytes=40 * 2**20
        ),
        name="reduce_all",
    )(packed, place)


def on_device(
    pixels,
    tile_counts,
    text_gaps,
    stem_weight,
    depth_weight,
    norm_gain,
    up_weight,
    down_weight,
    layer_scale,
    embed_grad,
):
    n_enc = lax.axis_size("enc")
    n_dec = lax.axis_size("dec")
    weights = (stem_weight, depth_weight, norm_gain, up_weight, down_weight, layer_scale)
    unit = n_enc * n_dec * 16
    packed_rows = -(-PACKED // unit) * unit
    grad, meta = gather(n_dec, embed_grad, tile_counts, text_gaps)
    place, packed = tower(packed_rows, pixels[0], meta, grad, weights)
    scale = 1.0 / math.sqrt(n_dec * n_enc * MEAN_TILES * FEAT_TILE)
    sequence, stem, depth, gain, up, down, layer = reduce_all(n_enc, n_dec, scale, packed, place)
    return (sequence, stem, depth, gain[0], up, down, layer[0])


def solution(mesh):
    return jax.shard_map(
        on_device,
        mesh=mesh,
        in_specs=(
            P("dec", "enc", None),
            P("dec", "enc"),
            P("dec", "enc"),
            P(),
            P(),
            P(),
            P(),
            P(),
            P(),
            P("enc", "dec", None),
        ),
        out_specs=(P("enc", "dec", None), P(), P(), P(), P(), P(), P()),
        check_vma=False,
    )
```

time: 235 us -> 75.4 us (0.32)
  waiting for transfers between devices: 89.3 us -> 0 us
  Pallas kernels: 0 us -> 59.8 us
  blocking collectives: 48.1 us -> 0 us
  other arithmetic: 35.5 us -> 1.19 us
  local copies, waits for them, and re-layouts: 32.3 us -> 11.6 us
  between operations: 17.3 us -> 1.97 us
  matrix products: 11.5 us -> 0 us
    psum x1 -> x0, waiting for transfers between devices: 89.3 us -> none  [on_device(): lax.psum((stem_term, depth_term, gain_term, up_term, down_term, scale_ter...]
    pallas_call x0 -> x3, Pallas kernels: none -> 59.8 us  [the longest x1 40.3 us: reduce_all(): pl.pallas_call(functools.partial(reduce_kernel, n_enc, n_dec, scale), out...]
    psum x1 -> x0, blocking collectives: 42 us -> none  [on_device(): lax.psum((stem_term, depth_term, gain_term, up_term, down_term, scale_ter...]
    another operation x51 -> x0, local copies, waits for them, and re-layouts: 25.1 us -> none  [the longest x50 23.4 us: backward_tail(): depth_term = jnp.stack(depth_rows)]
    reduce_sum x8 -> x0, other arithmetic: 15.3 us -> none  [the longest x1 6.67 us: encode(): channel_mean = jnp.mean(flat_rows, axis=1, keepdims=True)]
    dot_general x8 -> x0, matrix products: 11.5 us -> none  [the longest x1 1.99 us: backward_head(): lax.dot_general(activated, grad_proj, (((0,), (0,)), ((), ())), preferred...]
    mul x9 -> x0, other arithmetic: 8.94 us -> none  [the longest x1 2.38 us: on_device(): up_sum * grad_scale]
    unnamed x126 -> x19, local copies, waits for them, and re-layouts: 1.64 us -> 10.2 us
  transfers between devices with their start and end apart: 1 -> 0, of which waited for: 1 -> 0; matrix products, arithmetic and copies ran while one was open for 3% -> 0% of each run, Pallas kernels for 0% -> 0%
where the time goes in v1:
time: 75.4 us; the launch traced here: 74.5 us
  Pallas kernels  59.8 us (79%)
  local copies, waits for them, and re-layouts  11.6 us (15%)
  between operations  1.97 us (3%)
  other arithmetic  1.19 us (2%)
    pallas_call x1, Pallas kernels, reduce_all(): pl.pallas_call(functools.partial(reduce_kernel, n_enc, n_dec, scale), out...  40.3 us
    pallas_call x1, Pallas kernels, tower(): pl.pallas_call(functools.partial(tower_kernel, tiles), out_shape=(jax.Sha...  16.4 us
    unnamed x19, local copies, waits for them, and re-layouts  10.2 us
    pallas_call x1, Pallas kernels, gather(): pl.pallas_call(functools.partial(gather_kernel, n_dec), out_shape=(jax.Sh...  3.15 us

profile of v1, /device:TPU:0, one launch (start us, length us, event | category | flops | bytes accessed | tf_op | source)
XLA Modules:
  0.0 74.5 jit_solution(17408713920001358070)
XLA Ops:
  1.9 0.7 reshape.20.gain_ref
  2.6 0.7 reshape.21.layer_ref
  3.3 3.2 %gather_dec.1 = (bf16[416,384]{1,0:T(8,128)(2,1)}, s32[16,128]{1,0:T(8,128)}) custom-call(bf16[1,208,384]{2,1,0:T(8,128)(2,1)} %grad_ref.1, s32[1,1]{1,0:T(1,128)S(6)} %copy.22.count_ref, s32[1,1]{1,0:T(1,128)S(6)} %copy.23.gap_ref), custom_call_target="tpu_custom_call" | custom-call | tf_op jit(solution)/shard_map/gather_dec/pallas_call | solution.py:95
  6.5 0.0 copy-start
  6.5 1.1 %copy-done = bf16[384,768]{1,0:T(8,128)(2,1)S(1)} copy-done((bf16[384,768]{1,0:T(8,128)(2,1)S(1)}, bf16[384,768]{1,0:T(8,128)(2,1)}, u32[]{:S(2)}) %copy-start) | copy-done | bytes 589848
  7.5 0.0 copy-start.1
  7.5 1.1 %copy-done.1 = bf16[768,384]{1,0:T(8,128)(2,1)S(1)} copy-done((bf16[768,384]{1,0:T(8,128)(2,1)S(1)}, bf16[768,384]{1,0:T(8,128)(2,1)}, u32[]{:S(2)}) %copy-start.1) | copy-done | bytes 589848
  8.6 0.0 copy-start.2
  8.6 1.0 %copy-done.2 = bf16[416,384]{1,0:T(8,128)(2,1)S(1)} copy-done((bf16[416,384]{1,0:T(8,128)(2,1)S(1)}, bf16[416,384]{1,0:T(8,128)(2,1)}, u32[]{:S(2)}) %copy-start.2) | copy-done | bytes 319512
  9.6 0.0 copy-start.3
  9.6 0.9 %copy-done.3 = bf16[1,9,3072]{2,1,0:T(8,128)(2,1)S(1)} copy-done((bf16[1,9,3072]{2,1,0:T(8,128)(2,1)S(1)}, bf16[1,9,3072]{2,1,0:T(8,128)(2,1)}, u32[]{:S(2)}) %copy-start.3) | copy-done | bytes 55320
  10.4 0.0 copy-start.4
  10.5 0.8 %copy-done.4 = bf16[49,384]{1,0:T(8,128)(2,1)S(1)} copy-done((bf16[49,384]{1,0:T(8,128)(2,1)S(1)}, bf16[49,384]{1,0:T(8,128)(2,1)}, u32[]{:S(2)}) %copy-start.4) | copy-done | bytes 37656
  11.2 0.0 copy-start.5
  11.2 0.8 %copy-done.5 = bf16[48,384]{1,0:T(8,128)(2,1)S(1)} copy-done((bf16[48,384]{1,0:T(8,128)(2,1)S(1)}, bf16[48,384]{1,0:T(8,128)(2,1)}, u32[]{:S(2)}) %copy-start.5) | copy-done | bytes 36888
  12.0 0.0 copy-start.6
  12.0 0.7 copy-done.6
  12.7 16.4 %tower.1 = (bf16[416,384]{1,0:T(8,128)(2,1)S(1)}, bf16[5120,128]{1,0:T(8,128)(2,1)S(1)}) custom-call(bf16[9,3072]{1,0:T(8,128)(2,1)S(1)} %bitcast.1, s32[16,128]{1,0:T(8,128)S(1)} %copy-done.6, bf16[416,384]{1,0:T(8,128)(2,1)S(1)} %copy-done.2, bf16[48,384]{1,0:T(8,128)(2,1)S(1)} %copy-done.5, bf16[49,384]{1,0:T(8,128)(2,1)S(1)} %copy-done.4, ...), custom_call_target="tpu_custom_call" | custom-call | tf_op jit(solution)/shard_map/tower/pallas_call | solution.py:335
  29.1 40.3 %reduce_all.1 = (bf16[1,208,384]{2,1,0:T(8,128)(2,1)S(1)}, f32[48,384]{1,0:T(8,128)S(1)}, f32[49,384]{1,0:T(8,128)S(1)}, f32[1,384]{1,0:T(1,128)S(1)}, f32[384,7...) custom-call(bf16[5120,128]{1,0:T(8,128)(2,1)S(1)} %get-tuple-element.20.pack_ref, ...), custom_call_target="tpu_custom_call" | custom-call | tf_op jit(solution)/shard_map/reduce_all/pallas_call | solution.py:543
  69.4 0.6 reduce
  70.0 0.6 reduce.1
  70.6 0.7 copy.24
  71.2 0.6 copy.25
  71.9 0.6 copy.26
  72.5 1.0 %copy.27 = f32[384,768]{1,0:T(8,128)} copy(f32[384,768]{1,0:T(8,128)S(1)} %get-tuple-element.40) | data formatting | bytes 2359296
  73.5 1.0 %copy.28 = f32[768,384]{1,0:T(8,128)} copy(f32[768,384]{1,0:T(8,128)S(1)} %get-tuple-element.41) | data formatting | bytes 2359296
Async XLA Ops:
  6.5 1.1 %copy-start = (bf16[384,768]{1,0:T(8,128)(2,1)S(1)}, bf16[384,768]{1,0:T(8,128)(2,1)}, u32[]{:S(2)}) copy-start(bf16[384,768]{1,0:T(8,128)(2,1)} %up_ref.1) | copy-start | bytes 1769476
  7.5 1.1 %copy-start.1 = (bf16[768,384]{1,0:T(8,128)(2,1)S(1)}, bf16[768,384]{1,0:T(8,128)(2,1)}, u32[]{:S(2)}) copy-start(bf16[768,384]{1,0:T(8,128)(2,1)} %down_ref.1) | copy-start | bytes 1769476
  8.6 1.0 %copy-start.2 = (bf16[416,384]{1,0:T(8,128)(2,1)S(1)}, bf16[416,384]{1,0:T(8,128)(2,1)}, u32[]{:S(2)}) copy-start(bf16[416,384]{1,0:T(8,128)(2,1)} %get-tuple-element.19.grad_ref) | copy-start | bytes 958468
  9.6 0.9 %copy-start.3 = (bf16[1,9,3072]{2,1,0:T(8,128)(2,1)S(1)}, bf16[1,9,3072]{2,1,0:T(8,128)(2,1)}, u32[]{:S(2)}) copy-start(bf16[1,9,3072]{2,1,0:T(8,128)(2,1)} %param.10) | copy-start | bytes 165892
  10.4 0.8 %copy-start.4 = (bf16[49,384]{1,0:T(8,128)(2,1)S(1)}, bf16[49,384]{1,0:T(8,128)(2,1)}, u32[]{:S(2)}) copy-start(bf16[49,384]{1,0:T(8,128)(2,1)} %depth_ref.1) | copy-start | bytes 112900
  11.2 0.8 %copy-start.5 = (bf16[48,384]{1,0:T(8,128)(2,1)S(1)}, bf16[48,384]{1,0:T(8,128)(2,1)}, u32[]{:S(2)}) copy-start(bf16[48,384]{1,0:T(8,128)(2,1)} %stem_ref.1) | copy-start | bytes 110596
  12.0 0.7 copy-start.6

commit v2 on v1

v2 whole, which is shorter than its diff:
```python
import functools
import math

import jax
import jax.numpy as jnp
from jax import lax
from jax.experimental import pallas as pl
from jax.experimental.pallas import tpu as pltpu
from jax.sharding import PartitionSpec as P

WIDTH = 384
INNER = 768
KERNEL = 7
REACH = 3
PATCH_CH = 48
TILE = 8
MEAN_TILES = 3
FEAT_TILE = 16
LANES = 128
GROUPS = WIDTH // LANES
EPSILON = 1e-06
GELU_A = math.sqrt(2.0 / math.pi)
GELU_B = 0.044715
MESH = pl.DeviceIdType.MESH

UP_AT = 0
DOWN_AT = UP_AT + (INNER // LANES) * WIDTH
BIG = DOWN_AT + GROUPS * INNER
STEM_AT = 0
SMALL_AT = STEM_AT + GROUPS * PATCH_CH
SMALL = 64
LITTLE = SMALL_AT + GROUPS * SMALL
GAIN_ROW = 56
SCALE_ROW = 57
CHUNKS = 4

NT = (((1,), (1,)), ((), ()))
TN = (((0,), (0,)), ((), ()))


def dot(left, right, dims=(((1,), (0,)), ((), ()))):
    return lax.dot_general(left, right, dims, preferred_element_type=jnp.float32)


def vmem():
    return pl.BlockSpec(memory_space=pltpu.VMEM)


def whole_ref():
    return pl.BlockSpec(memory_space=pl.ANY)


def enc_digits(n_enc):
    sizes, left = ([2, 2, 4], 1) if n_enc == 16 else ([], n_enc)
    while left > 1:
        size = next((s for s in (4, 2, 3, 5, 7) if left % s == 0), left)
        sizes.append(size)
        left //= size
    digits, stride = [], 1
    for size in sizes:
        digits.append(("enc", stride, size))
        stride *= size
    return digits


def big_stages(n_enc, n_dec):
    digits = enc_digits(n_enc)
    return [s for s in [[("dec", 1, n_dec)], digits[:2], digits[2:]] if s]


def little_stages(n_enc, n_dec):
    digits = enc_digits(n_enc)
    return [s for s in [[("dec", 1, n_dec)] + digits[:2], digits[2:]] if s]


def stage_size(stage):
    return math.prod(size for _, _, size in stage)


def chunk_rows(n_enc, n_dec):
    unit = n_enc * n_dec * 16
    units = -(-BIG // unit)
    count = min(CHUNKS, units)
    return [unit * (units * (k + 1) // count - units * k // count) for k in range(count)]


class Route:
    def __init__(self, stage, enc_here, dec_here):
        here = {"enc": enc_here, "dec": dec_here}
        self.size = stage_size(stage)
        values = [lax.rem(lax.div(here[axis], stride), size) for axis, stride, size in stage]
        self.index, weight = 0, 1
        for value, (_, _, size) in zip(values, stage):
            self.index = self.index + value * weight
            weight *= size
        self.others, self.peers = [], []
        for step in range(1, self.size):
            other = lax.rem(self.index + step, self.size)
            self.others.append(other)
            place, left = dict(here), other
            for value, (axis, stride, size) in zip(values, stage):
                place[axis] = place[axis] + (lax.rem(left, size) - value) * stride
                left = lax.div(left, size)
            self.peers.append((place["enc"], place["dec"]))


def send(source, target, sems, number, peer):
    copy = pltpu.make_async_remote_copy(
        src_ref=source,
        dst_ref=target,
        send_sem=sems.at[number, 0],
        recv_sem=sems.at[number, 1],
        device_id=peer,
        device_id_type=MESH,
    )
    copy.start()
    return copy


class Sum:
    def __init__(self, routes, source, first, rows, target, landed, held, sems):
        self.routes, self.source, self.first, self.rows = routes, source, first, rows
        self.target, self.landed, self.held, self.sems = target, landed, held, sems
        self.number, self.at, self.height = 0, 0, rows
        self.offset, self.offsets, self.pending, self.sent = 0, [], [], []

    def done(self):
        return self.at > 2 * len(self.routes)

    def post(self, source, target, peer):
        copy = send(source, target, self.sems, self.number, peer)
        self.number += 1
        self.pending.append(copy)
        self.sent.append(copy)

    def advance(self):
        if self.done():
            return
        depth = len(self.routes)
        if 1 <= self.at <= depth:
            stage = self.at - 1
            route = self.routes[stage]
            part = self.height // route.size
            total = self.mine[
                pl.ds(pl.multiple_of(self.base + route.index * part, 16), part), :
            ].astype(jnp.float32)
            for step, copy in enumerate(self.pending):
                copy.wait_recv()
                total = total + self.landed[stage][step].astype(jnp.float32)
            self.offset = self.offset + route.index * part
            self.offsets.append(self.offset)
            self.height = part
            if stage < depth - 1:
                self.held[stage][...] = total.astype(jnp.bfloat16)
            else:
                rows = pl.ds(pl.multiple_of(self.first + self.offset, 16), part)
                self.target[rows, :] = total.astype(jnp.bfloat16)
        else:
            for copy in self.pending:
                copy.wait_recv()
            if self.at > depth:
                self.height *= self.routes[2 * depth - self.at].size
        self.pending = []
        if self.at < depth:
            route = self.routes[self.at]
            self.mine, self.base = (
                (self.source, self.first) if self.at == 0 else (self.held[self.at - 1], 0)
            )
            part = self.height // route.size
            for step, (other, peer) in enumerate(zip(route.others, route.peers)):
                rows = pl.ds(pl.multiple_of(self.base + other * part, 16), part)
                self.post(self.mine.at[rows], self.landed[self.at].at[step], peer)
        elif self.at < 2 * depth:
            stage = 2 * depth - 1 - self.at
            first = self.first + self.offsets[stage]
            rows = self.target.at[pl.ds(pl.multiple_of(first, 16), self.height)]
            for peer in self.routes[stage].peers:
                self.post(rows, rows, peer)
        self.at += 1

    def close(self):
        for copy in self.sent:
            copy.wait_send()


def sum_scratch(stages, rows):
    landed, held = [], []
    for stage in stages:
        size = stage_size(stage)
        rows //= size
        landed.append(pltpu.VMEM((max(size - 1, 1), rows, LANES), jnp.bfloat16))
        held.append(pltpu.VMEM((rows, LANES), jnp.bfloat16))
    steps = max(2 * sum(stage_size(stage) - 1 for stage in stages), 1)
    return landed + held + [pltpu.SemaphoreType.DMA((steps, 2))]


def shift_rows(value, amount):
    if amount == 0:
        return value
    row = lax.broadcasted_iota(jnp.int32, value.shape, 0)
    inside = (row + amount >= 0) & (row + amount < TILE)
    return jnp.where(inside, pltpu.roll(value, (-amount) % TILE, 0), 0.0)


def tower_kernel(n_enc, n_dec, tiles, *refs):
    (
        count_ref,
        gap_ref,
        pixels_any,
        stem_any,
        depth_any,
        gain_any,
        up_any,
        down_any,
        layer_any,
        grad_any,
        seq_ref,
        big_ref,
        little_ref,
        pixels_ref,
        stem_ref,
        depth_ref,
        gain_ref,
        up_ref,
        down_ref,
        layer_ref,
        grad_ref,
        info,
        load_sems,
        dec_sems,
        place_ref,
        place_in,
        big_pack,
        little_pack,
        wide,
        rows_in,
        stem_out,
        field,
        taps,
        normed_all,
        act_all,
        proj_all,
        hid_all,
        block_all,
        pool,
        depth_acc,
        small_acc,
    ) = refs[:41]
    spare = list(refs[41:])
    enc_here = lax.axis_index("enc")
    dec_here = lax.axis_index("dec")
    span = tiles * TILE
    chunk = 2 * span
    seq = grad_ref.shape[0]
    seq_rows = seq // n_dec

    big = [Route(stage, enc_here, dec_here) for stage in big_stages(n_enc, n_dec)]
    little = [Route(stage, enc_here, dec_here) for stage in little_stages(n_enc, n_dec)]
    across = Route([("dec", 1, n_dec)], enc_here, dec_here)

    def take(routes, *rest):
        depth = len(routes)
        landed, held, sems = spare[:depth], spare[depth : 2 * depth], spare[2 * depth]
        del spare[: 2 * depth + 1]
        return Sum(routes, *rest, landed, held, sems)

    sums, ready, first = [], [], 0
    for rows in chunk_rows(n_enc, n_dec):
        sums.append(take(big, big_pack, first, rows, big_ref))
        first += rows
        ready.append(first)
    last = take(little, little_pack, 0, little_pack.shape[0], little_ref)

    barrier = pltpu.get_barrier_semaphore()
    greeted = 0
    for route in little:
        for peer in route.peers:
            pl.semaphore_signal(barrier, inc=1, device_id=peer, device_id_type=MESH)
            greeted += 1
    own_rows = pl.ds(pl.multiple_of(dec_here * seq_rows, 16), seq_rows)
    loads = []
    for number, (source, target) in enumerate(
        (
            (pixels_any.at[0], pixels_ref),
            (stem_any, stem_ref),
            (depth_any, depth_ref),
            (gain_any, gain_ref.at[0]),
            (layer_any, layer_ref.at[0]),
            (up_any, up_ref),
            (down_any, down_ref),
            (grad_any.at[0], grad_ref.at[own_rows]),
        )
    ):
        copy = pltpu.make_async_copy(source, target, load_sems.at[number])
        copy.start()
        loads.append(copy)

    count_here = count_ref[0, 0]
    gap_here = gap_ref[0, 0]
    mine = pl.ds(pl.multiple_of(dec_here * 16, 16), 16)
    info[mine, :] = jnp.concatenate(
        [jnp.full((8, LANES), count_here, jnp.int32), jnp.full((8, LANES), gap_here, jnp.int32)],
        axis=0,
    )
    wide[...] = jnp.zeros_like(wide)
    for copy in loads[:3]:
        copy.wait()
    for col in range(TILE):
        wide[col * PATCH_CH : (col + 1) * PATCH_CH, col * WIDTH : (col + 1) * WIDTH] = stem_ref[...]
    for tap in range(KERNEL * KERNEL):
        taps[tap * 8 : tap * 8 + 8, :] = jnp.broadcast_to(
            depth_ref[tap : tap + 1, :].astype(jnp.float32), (8, WIDTH)
        )
    depth_acc[...] = jnp.zeros_like(depth_acc)
    small_acc[...] = jnp.zeros_like(small_acc)
    pix = pixels_ref[...].astype(jnp.float32)
    for tile in range(tiles):
        rows_in[tile * 8 : tile * 8 + 8, :] = jnp.concatenate(
            [pix[tile : tile + 1, r * WIDTH : (r + 1) * WIDTH] for r in range(TILE)], axis=0
        )
    rows = rows_in[...].astype(jnp.bfloat16)
    for col in range(TILE):
        stem_out[col * span : (col + 1) * span, :] = (
            dot(rows, wide[:, col * WIDTH : (col + 1) * WIDTH])
            .astype(jnp.bfloat16)
            .astype(jnp.float32)
        )

    def at(col, tile):
        return pl.ds(pl.multiple_of(col * span + tile * 8, 8), 8)

    def mix(tile, carry):
        for group in range(GROUPS):
            lanes = slice(group * LANES, (group + 1) * LANES)
            source = [stem_out[at(col, tile), lanes] for col in range(TILE)]
            total = [jnp.zeros((8, LANES), jnp.float32)] * TILE
            for a in range(KERNEL):
                moved = [shift_rows(value, a - REACH) for value in source]
                for b in range(KERNEL):
                    tap = a * KERNEL + b
                    weight = taps[tap * 8 : tap * 8 + 8, lanes]
                    for col in range(TILE):
                        other = col + b - REACH
                        if 0 <= other < TILE:
                            total[col] = total[col] + moved[other] * weight
            for col in range(TILE):
                field[at(col, tile), lanes] = total[col]
        return carry

    part = tiles * 2 // 3
    lax.fori_loop(0, part, mix, 0)
    pl.semaphore_wait(barrier, greeted)
    copies = []
    for step, peer in enumerate(across.peers):
        copies.append(send(info.at[mine], info.at[mine], dec_sems, 3 * step, peer))
        copies.append(send(grad_any.at[0], grad_ref.at[own_rows], dec_sems, 3 * step + 1, peer))
    lax.fori_loop(part, tiles, mix, 0)
    for copy in loads[3:]:
        copy.wait()
    for copy in copies:
        copy.wait()

    start = jnp.full((8, LANES), gap_here, jnp.int32)
    for other in range(n_dec):
        gone = info[other * 16 : other * 16 + 8, :] * FEAT_TILE
        gone = gone + info[other * 16 + 8 : other * 16 + 16, :]
        start = start + jnp.where(other < dec_here, gone, 0)
    start = start[0:1, 0:1]
    count = info[mine, :][0:1, 0:1]
    gain = gain_ref[...]
    layer = layer_ref[...]

    def fold(value):
        return jnp.sum(value.reshape(-1, 8, WIDTH), axis=0)

    def block(pair, carry):
        here = pl.ds(pl.multiple_of(pair * chunk, 16), chunk)
        mixed = field[here, :]
        dev = mixed - jnp.mean(mixed, axis=1, keepdims=True)
        inv = lax.rsqrt(jnp.mean(dev * dev, axis=1, keepdims=True) + EPSILON)
        centred = dev * inv
        normed = (centred * gain).astype(jnp.bfloat16)
        normed_all[here, :] = normed
        hidden = dot(normed, up_ref[...])
        square = hidden * hidden
        half = 0.5 + 0.5 * jnp.tanh(GELU_A * hidden * (1.0 + GELU_B * square))
        act = (hidden * half).astype(jnp.bfloat16)
        slope = half + hidden * (2.0 * half * (1.0 - half)) * (
            GELU_A + (3.0 * GELU_A * GELU_B) * square
        )
        act_all[here, :] = act
        projected = dot(act, down_ref[...])
        out = stem_out[here, :] + layer * projected
        both = out[:span] + out[span:]
        both = both + pltpu.roll(both, span - 1, 0)
        pool[pl.ds(pl.multiple_of(pair * span, 8), span), :] = 0.25 * both

        row = lax.broadcasted_iota(jnp.int32, (span, seq), 0)
        spot = lax.broadcasted_iota(jnp.int32, (span, seq), 1)
        tile = row // TILE
        want = start + tile * FEAT_TILE + (row % TILE) // 2 * 4 + pair
        pick = jnp.where((spot == want) & (tile < count), 0.25, 0.0).astype(jnp.bfloat16)
        once = dot(pick, grad_ref[...])
        grad_block = jnp.concatenate([once, once], axis=0)
        block_all[here, :] = grad_block
        small_acc[0:8, :] += fold(grad_block * projected)
        grad_proj = (grad_block * layer).astype(jnp.bfloat16)
        proj_all[here, :] = grad_proj
        grad_act = dot(grad_proj, down_ref[...], NT)
        grad_hidden = (grad_act * slope).astype(jnp.bfloat16)
        hid_all[here, :] = grad_hidden
        grad_normed = dot(grad_hidden, up_ref[...], NT)
        small_acc[8:16, :] += fold(grad_normed * centred)
        scaled = grad_normed * gain
        field[here, :] = inv * (
            scaled
            - jnp.mean(scaled, axis=1, keepdims=True)
            - centred * jnp.mean(scaled * centred, axis=1, keepdims=True)
        )
        return carry

    lax.fori_loop(0, TILE // 2, block, 0)

    place = jnp.zeros((seq, WIDTH), jnp.float32)
    for pair in range(TILE // 2):
        spot = lax.broadcasted_iota(jnp.int32, (seq, span), 0)
        row = lax.broadcasted_iota(jnp.int32, (seq, span), 1)
        tile = row // TILE
        want = start + tile * FEAT_TILE + (row % TILE) // 2 * 4 + pair
        hit = (spot == want) & (tile < count) & (row % 2 == 0)
        place = place + dot(
            jnp.where(hit, 1.0, 0.0).astype(jnp.bfloat16),
            pool[pair * span : (pair + 1) * span, :].astype(jnp.bfloat16),
        )
    place_ref[...] = place.astype(jnp.bfloat16)

    places = []
    for step, (other, peer) in enumerate(zip(across.others, across.peers)):
        rows_to = pl.ds(pl.multiple_of(other * seq_rows, 16), seq_rows)
        places.append(send(place_ref.at[rows_to], place_in.at[step], dec_sems, 3 * step + 2, peer))

    def pack(target, first, value):
        height = value.shape[0]
        for group in range(value.shape[1] // LANES):
            at_row = first + group * height
            target[at_row : at_row + height, :] = value[
                :, group * LANES : (group + 1) * LANES
            ].astype(jnp.bfloat16)

    def advance(filled):
        for one, end in zip(sums, ready):
            if end <= filled or filled == BIG:
                one.advance()

    if big_pack.shape[0] > BIG:
        big_pack[BIG:, :] = jnp.zeros((big_pack.shape[0] - BIG, LANES), jnp.bfloat16)
    pack(big_pack, UP_AT, dot(normed_all[...], hid_all[...], TN))
    advance(DOWN_AT)
    pack(big_pack, DOWN_AT, dot(act_all[...], proj_all[...], TN))
    advance(BIG)

    def unmix(tile, carry):
        for group in range(GROUPS):
            lanes = slice(group * LANES, (group + 1) * LANES)
            grads = [field[at(col, tile), lanes] for col in range(TILE)]
            source = [stem_out[at(col, tile), lanes] for col in range(TILE)]
            total = [block_all[at(col, tile), lanes] for col in range(TILE)]
            for a in range(KERNEL):
                moved = [shift_rows(value, REACH - a) for value in grads]
                for b in range(KERNEL):
                    tap = a * KERNEL + b
                    weight = taps[tap * 8 : tap * 8 + 8, lanes]
                    term = None
                    for col in range(TILE):
                        other = col - b + REACH
                        if 0 <= other < TILE:
                            total[col] = total[col] + moved[other] * weight
                            product = moved[other] * source[col]
                            term = product if term is None else term + product
                    depth_acc[tap * 8 : tap * 8 + 8, lanes] += term
            for col in range(TILE):
                block_all[at(col, tile), lanes] = total[col]
        return carry

    for third in range(3):
        lax.fori_loop(tiles * third // 3, tiles * (third + 1) // 3, unmix, 0)
        advance(BIG)

    stem_term = jnp.zeros((PATCH_CH, WIDTH), jnp.float32)
    for col in range(TILE):
        grad_stem = block_all[col * span : (col + 1) * span, :].astype(jnp.bfloat16)
        stem_term = (
            stem_term + dot(rows, grad_stem, TN)[col * PATCH_CH : (col + 1) * PATCH_CH, :]
        )
    pack(little_pack, STEM_AT, stem_term)
    taps_sum = jnp.sum(depth_acc[...].reshape(KERNEL * KERNEL, 8, WIDTH), axis=1)
    small = jnp.concatenate(
        [
            taps_sum,
            jnp.zeros((GAIN_ROW - KERNEL * KERNEL, WIDTH), jnp.float32),
            jnp.sum(small_acc[8:16, :], axis=0, keepdims=True),
            jnp.sum(small_acc[0:8, :], axis=0, keepdims=True),
            jnp.zeros((SMALL - SCALE_ROW - 1, WIDTH), jnp.float32),
        ],
        axis=0,
    )
    pack(little_pack, SMALL_AT, small)
    if little_pack.shape[0] > LITTLE:
        little_pack[LITTLE:, :] = jnp.zeros((little_pack.shape[0] - LITTLE, LANES), jnp.bfloat16)
    last.advance()

    sequence = place_ref[own_rows, :].astype(jnp.float32)
    for step, copy in enumerate(places):
        copy.wait_recv()
        sequence = sequence + place_in[step].astype(jnp.float32)
    seq_ref[...] = sequence.astype(jnp.bfloat16)
    while not (last.done() and all(one.done() for one in sums)):
        for one in sums:
            one.advance()
        last.advance()
    for one in [*sums, last]:
        one.close()
    for copy in places:
        copy.wait_send()


def tower(n_enc, n_dec, args):
    pixels, grad = args[2], args[-1]
    tiles = pixels.shape[1]
    positions = tiles * TILE * TILE
    span = tiles * TILE
    seq_rows = grad.shape[1]
    seq = n_dec * seq_rows
    f32, bf16 = jnp.float32, jnp.bfloat16
    chunks = chunk_rows(n_enc, n_dec)
    big_rows = sum(chunks)
    unit = n_enc * n_dec * 16
    little_rows = -(-LITTLE // unit) * unit
    steps = max(n_dec - 1, 1)
    smem = pl.BlockSpec(memory_space=pltpu.SMEM)
    scratch = [
        pltpu.VMEM((tiles, TILE * TILE * PATCH_CH), bf16),
        pltpu.VMEM((PATCH_CH, WIDTH), bf16),
        pltpu.VMEM((KERNEL * KERNEL, WIDTH), bf16),
        pltpu.VMEM((1, WIDTH), f32),
        pltpu.VMEM((WIDTH, INNER), bf16),
        pltpu.VMEM((INNER, WIDTH), bf16),
        pltpu.VMEM((1, WIDTH), f32),
        pltpu.VMEM((seq, WIDTH), bf16),
        pltpu.VMEM((n_dec * 16, LANES), jnp.int32),
        pltpu.SemaphoreType.DMA((8,)),
        pltpu.SemaphoreType.DMA((3 * steps, 2)),
        pltpu.VMEM((seq, WIDTH), bf16),
        pltpu.VMEM((steps, seq_rows, WIDTH), bf16),
        pltpu.VMEM((big_rows, LANES), bf16),
        pltpu.VMEM((little_rows, LANES), bf16),
        pltpu.VMEM((WIDTH, TILE * WIDTH), bf16),
        pltpu.VMEM((span, WIDTH), f32),
        pltpu.VMEM((positions, WIDTH), f32),
        pltpu.VMEM((positions, WIDTH), f32),
        pltpu.VMEM((KERNEL * KERNEL * 8, WIDTH), f32),
        pltpu.VMEM((positions, WIDTH), bf16),
        pltpu.VMEM((positions, INNER), bf16),
        pltpu.VMEM((positions, WIDTH), bf16),
        pltpu.VMEM((positions, INNER), bf16),
        pltpu.VMEM((positions, WIDTH), f32),
        pltpu.VMEM((positions // 2, WIDTH), f32),
        pltpu.VMEM((KERNEL * KERNEL * 8, WIDTH), f32),
        pltpu.VMEM((16, WIDTH), f32),
    ]
    for rows in chunks:
        scratch += sum_scratch(big_stages(n_enc, n_dec), rows)
    scratch += sum_scratch(little_stages(n_enc, n_dec), little_rows)
    return pl.pallas_call(
        functools.partial(tower_kernel, n_enc, n_dec, tiles),
        out_shape=(
            jax.ShapeDtypeStruct((seq_rows, WIDTH), bf16),
            jax.ShapeDtypeStruct((big_rows, LANES), bf16),
            jax.ShapeDtypeStruct((little_rows, LANES), bf16),
        ),
        in_specs=[smem, smem] + [whole_ref()] * 8,
        out_specs=(vmem(),) * 3,
        scratch_shapes=scratch,
        compiler_params=pltpu.CompilerParams(
            collective_id=0, has_side_effects=True, vmem_limit_bytes=56 * 2**20
        ),
        name="tower",
    )(*args)


def unpack_kernel(scale, seq_in, big, little, *refs):
    outs, holds, sems = refs[:7], refs[7:14], refs[14]
    seq_ref, stem_ref, depth_ref, gain_ref, up_ref, down_ref, scale_ref = holds
    copies = []

    def store(number):
        source, target = holds[number], outs[number]
        if number == 0:
            target = target.at[0]
        if number in (3, 6):
            source = source.at[0]
        copy = pltpu.make_async_copy(source, target, sems.at[number])
        copy.start()
        copies.append(copy)

    def unpack(source, first, rows, group):
        at_row = first + group * rows
        return source[at_row : at_row + rows, :].astype(jnp.float32) * scale

    for group in range(INNER // LANES):
        up_ref[:, group * LANES : (group + 1) * LANES] = unpack(big, UP_AT, WIDTH, group)
    store(4)
    for group in range(GROUPS):
        down_ref[:, group * LANES : (group + 1) * LANES] = unpack(big, DOWN_AT, INNER, group)
    store(5)
    seq_ref[...] = seq_in[...]
    store(0)
    for group in range(GROUPS):
        lanes = slice(group * LANES, (group + 1) * LANES)
        stem_ref[:, lanes] = unpack(little, STEM_AT, PATCH_CH, group)
        small = unpack(little, SMALL_AT, SMALL, group)
        depth_ref[:, lanes] = small[: KERNEL * KERNEL]
        gain_ref[:, lanes] = small[GAIN_ROW : GAIN_ROW + 1]
        scale_ref[:, lanes] = small[SCALE_ROW : SCALE_ROW + 1]
    for number in (1, 2, 3, 6):
        store(number)
    for copy in copies:
        copy.wait()


def unpack_all(scale, sequence, big, little):
    f32, bf16 = jnp.float32, jnp.bfloat16
    seq_rows = sequence.shape[0]
    shapes = [
        ((1, seq_rows, WIDTH), bf16),
        ((PATCH_CH, WIDTH), f32),
        ((KERNEL * KERNEL, WIDTH), f32),
        ((WIDTH,), f32),
        ((WIDTH, INNER), f32),
        ((INNER, WIDTH), f32),
        ((WIDTH,), f32),
    ]
    held = [(seq_rows, WIDTH)] + [s if len(s) == 2 else (1, WIDTH) for s, _ in shapes[1:]]
    return pl.pallas_call(
        functools.partial(unpack_kernel, scale),
        out_shape=tuple(jax.ShapeDtypeStruct(s, kind) for s, kind in shapes),
        in_specs=[vmem()] * 3,
        out_specs=(whole_ref(),) * 7,
        scratch_shapes=[pltpu.VMEM(s, kind) for s, (_, kind) in zip(held, shapes)]
        + [pltpu.SemaphoreType.DMA((7,))],
        compiler_params=pltpu.CompilerParams(vmem_limit_bytes=32 * 2**20),
        name="unpack",
    )(sequence, big, little)


def on_device(
    pixels,
    tile_counts,
    text_gaps,
    stem_weight,
    depth_weight,
    norm_gain,
    up_weight,
    down_weight,
    layer_scale,
    embed_grad,
):
    n_enc = lax.axis_size("enc")
    n_dec = lax.axis_size("dec")
    weights = (stem_weight, depth_weight, norm_gain, up_weight, down_weight, layer_scale)
    sequence, big, little = tower(
        n_enc, n_dec, (tile_counts, text_gaps, pixels, *weights, embed_grad)
    )
    scale = 1.0 / math.sqrt(n_dec * n_enc * MEAN_TILES * FEAT_TILE)
    return unpack_all(scale, sequence, big, little)


def solution(mesh):
    return jax.shard_map(
        on_device,
        mesh=mesh,
        in_specs=(
            P("dec", "enc", None),
            P("dec", "enc"),
            P("dec", "enc"),
            P(),
            P(),
            P(),
            P(),
            P(),
            P(),
            P("enc", "dec", None),
        ),
        out_specs=(P("enc", "dec", None), P(), P(), P(), P(), P(), P()),
        check_vma=False,
    )
```

time: 75.4 us -> 55.2 us (0.73)
  Pallas kernels: 59.8 us -> 49.9 us
  local copies, waits for them, and re-layouts: 11.6 us -> 3.08 us
  other arithmetic: 1.19 us -> 0 us
    pallas_call x3 -> x2, Pallas kernels: 59.8 us -> 49.9 us  [the longest x1 48.3 us: tower(): pl.pallas_call(functools.partial(tower_kernel, n_enc, n_dec, tiles), out_...]
    unnamed x19 -> x6, local copies, waits for them, and re-layouts: 10.2 us -> 3.08 us
    reshape x2 -> x0, local copies, waits for them, and re-layouts: 1.37 us -> none  [the longest x1 0.68 us: tower(): norm_gain.reshape(1, WIDTH)]
    pallas_call x2 -> x0, other arithmetic: 1.19 us -> none  [reduce_all(): pl.pallas_call(functools.partial(reduce_kernel, n_enc, n_dec, scale), out...]
where the time goes in v2:
time: 55.2 us; the launch traced here: 55 us
  Pallas kernels  49.9 us (90%)
  local copies, waits for them, and re-layouts  3.08 us (6%)
  between operations  1.94 us (4%)
    pallas_call x1, Pallas kernels, tower(): pl.pallas_call(functools.partial(tower_kernel, n_enc, n_dec, tiles), out_...  48.3 us
    unnamed x6, local copies, waits for them, and re-layouts  3.08 us
    pallas_call x1, Pallas kernels, unpack_all(): pl.pallas_call(functools.partial(unpack_kernel, scale), out_shape=tuple((...  1.64 us

profile of v2, /device:TPU:0, one launch (start us, length us, event | category | flops | bytes accessed | tf_op | source)
XLA Modules:
  0.0 55.0 jit_solution(8262773579427369786)
XLA Ops:
  1.9 48.3 %tower.1 = (bf16[208,384]{1,0:T(8,128)(2,1)}, bf16[4608,128]{1,0:T(8,128)(2,1)}, bf16[512,128]{1,0:T(8,128)(2,1)}) custom-call(s32[1,1]{1,0:T(1,128)S(6)} %copy.17.refs_0_, s32[1,1]{1,0:T(1,128)S(6)} %copy.18.refs_1_, bf16[1,9,3072]{2,1,0:T(8,128)(2,1)} %refs_2_.1, bf16[48,384]{1,0:T(8,128)(2,1)} %refs_3_.1, bf16[49,384]{1,0:T(8,128)(2,1)} %refs_4_.1, ...), custom_call_target="tpu_custom_call" | custom-call | tf_op jit(solution)/shard_map/tower/pallas_call | solution.py:574
  50.2 0.0 copy-start
  50.2 1.3 %copy-done = bf16[4608,128]{1,0:T(8,128)(2,1)S(1)} copy-done((bf16[4608,128]{1,0:T(8,128)(2,1)S(1)}, bf16[4608,128]{1,0:T(8,128)(2,1)}, u32[]{:S(2)}) %copy-start) | copy-done | bytes 1179672
  51.5 0.0 copy-start.1
  51.5 0.9 %copy-done.1 = bf16[208,384]{1,0:T(8,128)(2,1)S(1)} copy-done((bf16[208,384]{1,0:T(8,128)(2,1)S(1)}, bf16[208,384]{1,0:T(8,128)(2,1)}, u32[]{:S(2)}) %copy-start.1) | copy-done | bytes 159768
  52.4 0.0 copy-start.2
  52.4 0.9 %copy-done.2 = bf16[512,128]{1,0:T(8,128)(2,1)S(1)} copy-done((bf16[512,128]{1,0:T(8,128)(2,1)S(1)}, bf16[512,128]{1,0:T(8,128)(2,1)}, u32[]{:S(2)}) %copy-start.2) | copy-done | bytes 131096
  53.3 1.6 %unpack.1 = (bf16[1,208,384]{2,1,0:T(8,128)(2,1)}, f32[48,384]{1,0:T(8,128)}, f32[49,384]{1,0:T(8,128)}, f32[384]{0:T(512)}, f32[384,768]{1,0:T(8,128)}, /*index=5*/f32[768,384]{1,0:T(8,128)}, f32[384]{0:T(512)}) custom-call(bf16[208,384]{1,0:T(8,128)(2,1)S(1)} %copy-done.1, bf16[4608,128]{1,0:T(8,128)(2,1)S(1)} %copy-done, bf16[512,128]{1,0:T(8,128)(2,1)S(1)} %copy-done.2), custom_call_target="tpu_custom_call" | custom-call | tf_op jit(solution)/shard_map/unpack/pallas_call | solution.py:644
Async XLA Ops:
  50.2 1.3 %copy-start = (bf16[4608,128]{1,0:T(8,128)(2,1)S(1)}, bf16[4608,128]{1,0:T(8,128)(2,1)}, u32[]{:S(2)}) copy-start(bf16[4608,128]{1,0:T(8,128)(2,1)} %get-tuple-element.11.big) | copy-start | bytes 3538948
  51.5 0.9 %copy-start.1 = (bf16[208,384]{1,0:T(8,128)(2,1)S(1)}, bf16[208,384]{1,0:T(8,128)(2,1)}, u32[]{:S(2)}) copy-start(bf16[208,384]{1,0:T(8,128)(2,1)} %get-tuple-element.10.seq_in) | copy-start | bytes 479236
  52.4 0.9 %copy-start.2 = (bf16[512,128]{1,0:T(8,128)(2,1)S(1)}, bf16[512,128]{1,0:T(8,128)(2,1)}, u32[]{:S(2)}) copy-start(bf16[512,128]{1,0:T(8,128)(2,1)} %get-tuple-element.12.little) | copy-start | bytes 393220

commit v3 on v2

--- a/solution.py
+++ b/solution.py
@@ -42,10 +42,6 @@
     return lax.dot_general(left, right, dims, preferred_element_type=jnp.float32)
 
 
-def vmem():
-    return pl.BlockSpec(memory_space=pltpu.VMEM)
-
-
 def whole_ref():
     return pl.BlockSpec(memory_space=pl.ANY)
 
@@ -63,9 +59,13 @@
     return digits
 
 
-def big_stages(n_enc, n_dec):
+def big_stages(n_enc, n_dec, odd=0):
     digits = enc_digits(n_enc)
-    return [s for s in [[("dec", 1, n_dec)], digits[:2], digits[2:]] if s]
+    if len(digits) > 1 and digits[0][2] == digits[1][2]:
+        (_, one, size), (_, two, _) = digits[:2]
+        lead = one + (two - one) * odd
+        digits[:2] = [("enc", lead, size), ("enc", one + two - lead, size)]
+    return [[("dec", 1, n_dec)]] + [[digit] for digit in digits]
 
 
 def little_stages(n_enc, n_dec):
@@ -214,9 +214,9 @@
         down_any,
         layer_any,
         grad_any,
-        seq_ref,
-        big_ref,
-        little_ref,
+        seq_any,
+        big_any,
+        little_any,
         pixels_ref,
         stem_ref,
         depth_ref,
@@ -245,8 +245,12 @@
         pool,
         depth_acc,
         small_acc,
-    ) = refs[:41]
-    spare = list(refs[41:])
+        seq_ref,
+        big_ref,
+        little_ref,
+        store_sems,
+    ) = refs[:45]
+    spare = list(refs[45:])
     enc_here = lax.axis_index("enc")
     dec_here = lax.axis_index("dec")
     span = tiles * TILE
@@ -254,7 +258,8 @@
     seq = grad_ref.shape[0]
     seq_rows = seq // n_dec
 
-    big = [Route(stage, enc_here, dec_here) for stage in big_stages(n_enc, n_dec)]
+    odd = lax.rem(dec_here, 2)
+    big = [Route(stage, enc_here, dec_here) for stage in big_stages(n_enc, n_dec, odd)]
     little = [Route(stage, enc_here, dec_here) for stage in little_stages(n_enc, n_dec)]
     across = Route([("dec", 1, n_dec)], enc_here, dec_here)
 
@@ -421,6 +426,26 @@
 
     lax.fori_loop(0, TILE // 2, block, 0)
 
+    def pack(target, first, value):
+        height = value.shape[0]
+        for group in range(value.shape[1] // LANES):
+            at_row = first + group * height
+            target[at_row : at_row + height, :] = value[
+                :, group * LANES : (group + 1) * LANES
+            ].astype(jnp.bfloat16)
+
+    def advance(filled):
+        for one, end in zip(sums, ready):
+            if end <= filled or filled == BIG:
+                one.advance()
+
+    if big_pack.shape[0] > BIG:
+        big_pack[BIG:, :] = jnp.zeros((big_pack.shape[0] - BIG, LANES), jnp.bfloat16)
+    pack(big_pack, UP_AT, dot(normed_all[...], hid_all[...], TN))
+    advance(DOWN_AT)
+    pack(big_pack, DOWN_AT, dot(act_all[...], proj_all[...], TN))
+    advance(BIG)
+
     place = jnp.zeros((seq, WIDTH), jnp.float32)
     for pair in range(TILE // 2):
         spot = lax.broadcasted_iota(jnp.int32, (seq, span), 0)
@@ -438,26 +463,6 @@
     for step, (other, peer) in enumerate(zip(across.others, across.peers)):
         rows_to = pl.ds(pl.multiple_of(other * seq_rows, 16), seq_rows)
         places.append(send(place_ref.at[rows_to], place_in.at[step], dec_sems, 3 * step + 2, peer))
-
-    def pack(target, first, value):
-        height = value.shape[0]
-        for group in range(value.shape[1] // LANES):
-            at_row = first + group * height
-            target[at_row : at_row + height, :] = value[
-                :, group * LANES : (group + 1) * LANES
-            ].astype(jnp.bfloat16)
-
-    def advance(filled):
-        for one, end in zip(sums, ready):
-            if end <= filled or filled == BIG:
-                one.advance()
-
-    if big_pack.shape[0] > BIG:
-        big_pack[BIG:, :] = jnp.zeros((big_pack.shape[0] - BIG, LANES), jnp.bfloat16)
-    pack(big_pack, UP_AT, dot(normed_all[...], hid_all[...], TN))
-    advance(DOWN_AT)
-    pack(big_pack, DOWN_AT, dot(act_all[...], proj_all[...], TN))
-    advance(BIG)
 
     def unmix(tile, carry):
         for group in range(GROUPS):
@@ -514,12 +519,29 @@
         copy.wait_recv()
         sequence = sequence + place_in[step].astype(jnp.float32)
     seq_ref[...] = sequence.astype(jnp.bfloat16)
+    stores = []
+
+    def store(source, target):
+        copy = pltpu.make_async_copy(source, target, store_sems.at[len(stores)])
+        copy.start()
+        stores.append(copy)
+
+    store(seq_ref, seq_any)
     while not (last.done() and all(one.done() for one in sums)):
-        for one in sums:
-            one.advance()
-        last.advance()
+        for one, end in zip(sums, ready):
+            if not one.done():
+                one.advance()
+                if one.done():
+                    rows = slice(one.first, end)
+                    store(big_ref.at[rows], big_any.at[rows])
+        if not last.done():
+            last.advance()
+            if last.done():
+                store(little_ref, little_any)
     for one in [*sums, last]:
         one.close()
+    for copy in stores:
+        copy.wait()
     for copy in places:
         copy.wait_send()
 
@@ -567,6 +589,10 @@
         pltpu.VMEM((positions // 2, WIDTH), f32),
         pltpu.VMEM((KERNEL * KERNEL * 8, WIDTH), f32),
         pltpu.VMEM((16, WIDTH), f32),
+        pltpu.VMEM((seq_rows, WIDTH), bf16),
+        pltpu.VMEM((big_rows, LANES), bf16),
+        pltpu.VMEM((little_rows, LANES), bf16),
+        pltpu.SemaphoreType.DMA((len(chunks) + 2,)),
     ]
     for rows in chunks:
         scratch += sum_scratch(big_stages(n_enc, n_dec), rows)
@@ -579,7 +605,7 @@
             jax.ShapeDtypeStruct((little_rows, LANES), bf16),
         ),
         in_specs=[smem, smem] + [whole_ref()] * 8,
-        out_specs=(vmem(),) * 3,
+        out_specs=(whole_ref(),) * 3,
         scratch_shapes=scratch,
         compiler_params=pltpu.CompilerParams(
             collective_id=0, has_side_effects=True, vmem_limit_bytes=56 * 2**20
@@ -588,10 +614,22 @@
     )(*args)
 
 
-def unpack_kernel(scale, seq_in, big, little, *refs):
+def unpack_kernel(scale, seq_any, big_any, little_any, *refs):
     outs, holds, sems = refs[:7], refs[7:14], refs[14]
+    big, little = refs[15:]
     seq_ref, stem_ref, depth_ref, gain_ref, up_ref, down_ref, scale_ref = holds
-    copies = []
+    copies, loads = [], []
+    for number, (source, target) in enumerate(
+        (
+            (big_any.at[UP_AT:DOWN_AT], big.at[UP_AT:DOWN_AT]),
+            (big_any.at[DOWN_AT:BIG], big.at[DOWN_AT:BIG]),
+            (seq_any, seq_ref),
+            (little_any, little),
+        )
+    ):
+        copy = pltpu.make_async_copy(source, target, sems.at[7 + number])
+        copy.start()
+        loads.append(copy)
 
     def store(number):
         source, target = holds[number], outs[number]
@@ -607,14 +645,17 @@
         at_row = first + group * rows
         return source[at_row : at_row + rows, :].astype(jnp.float32) * scale
 
+    loads[0].wait()
     for group in range(INNER // LANES):
         up_ref[:, group * LANES : (group + 1) * LANES] = unpack(big, UP_AT, WIDTH, group)
     store(4)
+    loads[1].wait()
     for group in range(GROUPS):
         down_ref[:, group * LANES : (group + 1) * LANES] = unpack(big, DOWN_AT, INNER, group)
     store(5)
-    seq_ref[...] = seq_in[...]
+    loads[2].wait()
     store(0)
+    loads[3].wait()
     for group in range(GROUPS):
         lanes = slice(group * LANES, (group + 1) * LANES)
         stem_ref[:, lanes] = unpack(little, STEM_AT, PATCH_CH, group)
@@ -644,11 +685,15 @@
     return pl.pallas_call(
         functools.partial(unpack_kernel, scale),
         out_shape=tuple(jax.ShapeDtypeStruct(s, kind) for s, kind in shapes),
-        in_specs=[vmem()] * 3,
+        in_specs=[pl.BlockSpec(memory_space=pltpu.HBM)] * 3,
         out_specs=(whole_ref(),) * 7,
         scratch_shapes=[pltpu.VMEM(s, kind) for s, (_, kind) in zip(held, shapes)]
-        + [pltpu.SemaphoreType.DMA((7,))],
-        compiler_params=pltpu.CompilerParams(vmem_limit_bytes=32 * 2**20),
+        + [
+            pltpu.SemaphoreType.DMA((11,)),
+            pltpu.VMEM(big.shape, bf16),
+            pltpu.VMEM(little.shape, bf16),
+        ],
+        compiler_params=pltpu.CompilerParams(vmem_limit_bytes=56 * 2**20),
         name="unpack",
     )(sequence, big, little)
 

time: 55.2 us -> 49.8 us (0.902)
  local copies, waits for them, and re-layouts: 3.08 us -> 0 us
  Pallas kernels: 49.9 us -> 47.7 us
    pallas_call x1, Pallas kernels: 48.3 us -> 44.9 us  [tower(): pl.pallas_call(functools.partial(tower_kernel, n_enc, n_dec, tiles), out_...]
    unnamed x6 -> x0, local copies, waits for them, and re-layouts: 3.08 us -> none
    pallas_call x1, Pallas kernels: 1.64 us -> 2.75 us  [unpack_all(): pl.pallas_call(functools.partial(unpack_kernel, scale), out_shape=tuple((...]
where the time goes in v3:
time: 49.8 us; the launch traced here: 49.6 us
  Pallas kernels  47.7 us (96%)
  between operations  1.93 us (4%)
    pallas_call x1, Pallas kernels, tower(): pl.pallas_call(functools.partial(tower_kernel, n_enc, n_dec, tiles), out_...  44.9 us
    pallas_call x1, Pallas kernels, unpack_all(): pl.pallas_call(functools.partial(unpack_kernel, scale), out_shape=tuple((...  2.75 us

profile of v3, /device:TPU:0, one launch (start us, length us, event | category | flops | bytes accessed | tf_op | source)
XLA Modules:
  0.0 49.6 jit_solution(4698046208778132599)
XLA Ops:
  1.9 44.9 %tower.1 = (bf16[208,384]{1,0:T(8,128)(2,1)}, bf16[4608,128]{1,0:T(8,128)(2,1)}, bf16[512,128]{1,0:T(8,128)(2,1)}) custom-call(s32[1,1]{1,0:T(1,128)S(6)} %copy.17.refs_0_, s32[1,1]{1,0:T(1,128)S(6)} %copy.18.refs_1_, bf16[1,9,3072]{2,1,0:T(8,128)(2,1)} %refs_2_.1, bf16[48,384]{1,0:T(8,128)(2,1)} %refs_3_.1, bf16[49,384]{1,0:T(8,128)(2,1)} %refs_4_.1, ...), custom_call_target="tpu_custom_call" | custom-call | tf_op jit(solution)/shard_map/tower/pallas_call | solution.py:600
  46.9 2.7 %unpack.1 = (bf16[1,208,384]{2,1,0:T(8,128)(2,1)}, f32[48,384]{1,0:T(8,128)}, f32[49,384]{1,0:T(8,128)}, f32[384]{0:T(512)}, f32[384,768]{1,0:T(8,128)}, /*index=5*/f32[768,384]{1,0:T(8,128)}, f32[384]{0:T(512)}) custom-call(bf16[208,384]{1,0:T(8,128)(2,1)} %get-tuple-element.10.seq_any, bf16[4608,128]{1,0:T(8,128)(2,1)} %get-tuple-element.11.big_any, ...), custom_call_target="tpu_custom_call" | custom-call | tf_op jit(solution)/shard_map/unpack/pallas_call | solution.py:685

commit v4 on v3

--- a/solution.py
+++ b/solution.py
@@ -259,7 +259,10 @@
     seq_rows = seq // n_dec
 
     odd = lax.rem(dec_here, 2)
-    big = [Route(stage, enc_here, dec_here) for stage in big_stages(n_enc, n_dec, odd)]
+    ways = [
+        [Route(stage, enc_here, dec_here) for stage in big_stages(n_enc, n_dec, turn)]
+        for turn in (odd, 1 - odd)
+    ]
     little = [Route(stage, enc_here, dec_here) for stage in little_stages(n_enc, n_dec)]
     across = Route([("dec", 1, n_dec)], enc_here, dec_here)
 
@@ -270,8 +273,8 @@
         return Sum(routes, *rest, landed, held, sems)
 
     sums, ready, first = [], [], 0
-    for rows in chunk_rows(n_enc, n_dec):
-        sums.append(take(big, big_pack, first, rows, big_ref))
+    for number, rows in enumerate(chunk_rows(n_enc, n_dec)):
+        sums.append(take(ways[number % 2], big_pack, first, rows, big_ref))
         first += rows
         ready.append(first)
     last = take(little, little_pack, 0, little_pack.shape[0], little_ref)
@@ -618,54 +621,44 @@
     outs, holds, sems = refs[:7], refs[7:14], refs[14]
     big, little = refs[15:]
     seq_ref, stem_ref, depth_ref, gain_ref, up_ref, down_ref, scale_ref = holds
-    copies, loads = [], []
-    for number, (source, target) in enumerate(
-        (
-            (big_any.at[UP_AT:DOWN_AT], big.at[UP_AT:DOWN_AT]),
-            (big_any.at[DOWN_AT:BIG], big.at[DOWN_AT:BIG]),
-            (seq_any, seq_ref),
-            (little_any, little),
-        )
-    ):
-        copy = pltpu.make_async_copy(source, target, sems.at[7 + number])
+    strips = [(UP_AT + k * WIDTH, WIDTH, 4, k) for k in range(INNER // LANES)]
+    strips += [(DOWN_AT + k * INNER, INNER, 5, k) for k in range(GROUPS)]
+    count = [0]
+
+    def move(source, target):
+        copy = pltpu.make_async_copy(source, target, sems.at[count[0]])
         copy.start()
-        loads.append(copy)
-
-    def store(number):
-        source, target = holds[number], outs[number]
-        if number == 0:
-            target = target.at[0]
-        if number in (3, 6):
-            source = source.at[0]
-        copy = pltpu.make_async_copy(source, target, sems.at[number])
-        copy.start()
-        copies.append(copy)
-
-    def unpack(source, first, rows, group):
-        at_row = first + group * rows
-        return source[at_row : at_row + rows, :].astype(jnp.float32) * scale
-
-    loads[0].wait()
-    for group in range(INNER // LANES):
-        up_ref[:, group * LANES : (group + 1) * LANES] = unpack(big, UP_AT, WIDTH, group)
-    store(4)
-    loads[1].wait()
-    for group in range(GROUPS):
-        down_ref[:, group * LANES : (group + 1) * LANES] = unpack(big, DOWN_AT, INNER, group)
-    store(5)
-    loads[2].wait()
-    store(0)
-    loads[3].wait()
+        count[0] += 1
+        return copy
+
+    loads = [
+        move(big_any.at[first : first + rows], big.at[first : first + rows])
+        for first, rows, _, _ in strips
+    ]
+    small_load = move(little_any, little)
+    stores = [move(seq_any, outs[0].at[0])]
+
+    def unpack(source, first, rows):
+        return source[first : first + rows, :].astype(jnp.float32) * scale
+
+    for load, (first, rows, number, group) in zip(loads, strips):
+        lanes = slice(group * LANES, (group + 1) * LANES)
+        load.wait()
+        holds[number][:, lanes] = unpack(big, first, rows)
+        stores.append(move(holds[number].at[:, lanes], outs[number].at[:, lanes]))
+    small_load.wait()
     for group in range(GROUPS):
         lanes = slice(group * LANES, (group + 1) * LANES)
-        stem_ref[:, lanes] = unpack(little, STEM_AT, PATCH_CH, group)
-        small = unpack(little, SMALL_AT, SMALL, group)
+        stem_ref[:, lanes] = unpack(little, STEM_AT + group * PATCH_CH, PATCH_CH)
+        small = unpack(little, SMALL_AT + group * SMALL, SMALL)
         depth_ref[:, lanes] = small[: KERNEL * KERNEL]
         gain_ref[:, lanes] = small[GAIN_ROW : GAIN_ROW + 1]
         scale_ref[:, lanes] = small[SCALE_ROW : SCALE_ROW + 1]
-    for number in (1, 2, 3, 6):
-        store(number)
-    for copy in copies:
+    for number in (1, 2):
+        stores.append(move(holds[number], outs[number]))
+    for number in (3, 6):
+        stores.append(move(holds[number].at[0], outs[number]))
+    for copy in stores:
         copy.wait()
 
 
@@ -689,7 +682,7 @@
         out_specs=(whole_ref(),) * 7,
         scratch_shapes=[pltpu.VMEM(s, kind) for s, (_, kind) in zip(held, shapes)]
         + [
-            pltpu.SemaphoreType.DMA((11,)),
+            pltpu.SemaphoreType.DMA((24,)),
             pltpu.VMEM(big.shape, bf16),
             pltpu.VMEM(little.shape, bf16),
         ],

time: 49.8 us -> 52.8 us (1.060)
  Pallas kernels: 47.7 us -> 50.4 us
    pallas_call x1, Pallas kernels: 2.75 us -> 6.19 us  [unpack_all(): pl.pallas_call(functools.partial(unpack_kernel, scale), out_shape=tuple((...]
    pallas_call x1, Pallas kernels: 44.9 us -> 44.2 us  [tower(): pl.pallas_call(functools.partial(tower_kernel, n_enc, n_dec, tiles), out_...]
where the time goes in v4:
time: 52.8 us; the launch traced here: 52.3 us
  Pallas kernels  50.4 us (95%)
  between operations  1.93 us (4%)
    pallas_call x1, Pallas kernels, tower(): pl.pallas_call(functools.partial(tower_kernel, n_enc, n_dec, tiles), out_...  44.2 us
    pallas_call x1, Pallas kernels, unpack_all(): pl.pallas_call(functools.partial(unpack_kernel, scale), out_shape=tuple((...  6.19 us

profile of v4, /device:TPU:0, one launch (start us, length us, event | category | flops | bytes accessed | tf_op | source)
XLA Modules:
  0.0 52.3 jit_solution(15724653770133318389)
XLA Ops:
  1.9 44.2 %tower.1 = (bf16[208,384]{1,0:T(8,128)(2,1)}, bf16[4608,128]{1,0:T(8,128)(2,1)}, bf16[512,128]{1,0:T(8,128)(2,1)}) custom-call(s32[1,1]{1,0:T(1,128)S(6)} %copy.17.refs_0_, s32[1,1]{1,0:T(1,128)S(6)} %copy.18.refs_1_, bf16[1,9,3072]{2,1,0:T(8,128)(2,1)} %refs_2_.1, bf16[48,384]{1,0:T(8,128)(2,1)} %refs_3_.1, bf16[49,384]{1,0:T(8,128)(2,1)} %refs_4_.1, ...), custom_call_target="tpu_custom_call" | custom-call | tf_op jit(solution)/shard_map/tower/pallas_call | solution.py:603
  46.1 6.2 %unpack.1 = (bf16[1,208,384]{2,1,0:T(8,128)(2,1)}, f32[48,384]{1,0:T(8,128)}, f32[49,384]{1,0:T(8,128)}, f32[384]{0:T(512)}, f32[384,768]{1,0:T(8,128)}, /*index=5*/f32[768,384]{1,0:T(8,128)}, f32[384]{0:T(512)}) custom-call(bf16[208,384]{1,0:T(8,128)(2,1)} %get-tuple-element.10.seq_any, bf16[4608,128]{1,0:T(8,128)(2,1)} %get-tuple-element.11.big_any, ...), custom_call_target="tpu_custom_call" | custom-call | tf_op jit(solution)/shard_map/unpack/pallas_call | solution.py:678

commit v5 on v3

--- a/solution.py
+++ b/solution.py
@@ -259,7 +259,10 @@
     seq_rows = seq // n_dec
 
     odd = lax.rem(dec_here, 2)
-    big = [Route(stage, enc_here, dec_here) for stage in big_stages(n_enc, n_dec, odd)]
+    ways = [
+        [Route(stage, enc_here, dec_here) for stage in big_stages(n_enc, n_dec, turn)]
+        for turn in (odd, 1 - odd)
+    ]
     little = [Route(stage, enc_here, dec_here) for stage in little_stages(n_enc, n_dec)]
     across = Route([("dec", 1, n_dec)], enc_here, dec_here)
 
@@ -270,8 +273,8 @@
         return Sum(routes, *rest, landed, held, sems)
 
     sums, ready, first = [], [], 0
-    for rows in chunk_rows(n_enc, n_dec):
-        sums.append(take(big, big_pack, first, rows, big_ref))
+    for number, rows in enumerate(chunk_rows(n_enc, n_dec)):
+        sums.append(take(ways[number % 2], big_pack, first, rows, big_ref))
         first += rows
         ready.append(first)
     last = take(little, little_pack, 0, little_pack.shape[0], little_ref)
@@ -434,17 +437,26 @@
                 :, group * LANES : (group + 1) * LANES
             ].astype(jnp.bfloat16)
 
-    def advance(filled):
+    def begin(filled):
         for one, end in zip(sums, ready):
-            if end <= filled or filled == BIG:
+            if one.at == 0 and (end <= filled or filled == BIG):
                 one.advance()
+
+    def advance(ones):
+        for one in ones:
+            one.advance()
 
     if big_pack.shape[0] > BIG:
         big_pack[BIG:, :] = jnp.zeros((big_pack.shape[0] - BIG, LANES), jnp.bfloat16)
-    pack(big_pack, UP_AT, dot(normed_all[...], hid_all[...], TN))
-    advance(DOWN_AT)
+    normed_t = normed_all[...].T
+    pack(big_pack, UP_AT, dot(normed_t, hid_all[:, :WIDTH]))
+    begin(DOWN_AT // 2)
+    pack(big_pack, DOWN_AT // 2, dot(normed_t, hid_all[:, WIDTH:]))
+    begin(DOWN_AT)
+    early = [one for one in sums if one.at > 0]
     pack(big_pack, DOWN_AT, dot(act_all[...], proj_all[...], TN))
-    advance(BIG)
+    begin(BIG)
+    advance(early)
 
     place = jnp.zeros((seq, WIDTH), jnp.float32)
     for pair in range(TILE // 2):
@@ -489,7 +501,7 @@
 
     for third in range(3):
         lax.fori_loop(tiles * third // 3, tiles * (third + 1) // 3, unmix, 0)
-        advance(BIG)
+        advance(sums)
 
     stem_term = jnp.zeros((PATCH_CH, WIDTH), jnp.float32)
     for col in range(TILE):
@@ -627,17 +639,19 @@
             (little_any, little),
         )
     ):
-        copy = pltpu.make_async_copy(source, target, sems.at[7 + number])
+        copy = pltpu.make_async_copy(source, target, sems.at[number])
         copy.start()
         loads.append(copy)
 
-    def store(number):
+    def store(number, rows=None):
         source, target = holds[number], outs[number]
         if number == 0:
             target = target.at[0]
         if number in (3, 6):
             source = source.at[0]
-        copy = pltpu.make_async_copy(source, target, sems.at[number])
+        if rows is not None:
+            source, target = source.at[rows], target.at[rows]
+        copy = pltpu.make_async_copy(source, target, sems.at[4 + len(copies)])
         copy.start()
         copies.append(copy)
 
@@ -645,14 +659,21 @@
         at_row = first + group * rows
         return source[at_row : at_row + rows, :].astype(jnp.float32) * scale
 
+    def halves(number, first, rows, groups):
+        part = rows // 2
+        for half in range(2):
+            here = slice(half * part, (half + 1) * part)
+            for group in range(groups):
+                at_row = first + group * rows + half * part
+                holds[number][here, group * LANES : (group + 1) * LANES] = unpack(
+                    big, at_row, part, 0
+                )
+            store(number, here)
+
     loads[0].wait()
-    for group in range(INNER // LANES):
-        up_ref[:, group * LANES : (group + 1) * LANES] = unpack(big, UP_AT, WIDTH, group)
-    store(4)
+    halves(4, UP_AT, WIDTH, INNER // LANES)
     loads[1].wait()
-    for group in range(GROUPS):
-        down_ref[:, group * LANES : (group + 1) * LANES] = unpack(big, DOWN_AT, INNER, group)
-    store(5)
+    halves(5, DOWN_AT, INNER, GROUPS)
     loads[2].wait()
     store(0)
     loads[3].wait()
@@ -689,7 +710,7 @@
         out_specs=(whole_ref(),) * 7,
         scratch_shapes=[pltpu.VMEM(s, kind) for s, (_, kind) in zip(held, shapes)]
         + [
-            pltpu.SemaphoreType.DMA((11,)),
+            pltpu.SemaphoreType.DMA((24,)),
             pltpu.VMEM(big.shape, bf16),
             pltpu.VMEM(little.shape, bf16),
         ],

time: 49.8 us -> 49.4 us (level)
  Pallas kernels: 47.7 us -> 47 us
    pallas_call x1, Pallas kernels: 44.9 us -> 44.2 us  [tower(): pl.pallas_call(functools.partial(tower_kernel, n_enc, n_dec, tiles), out_...]
where the time goes in v5:
time: 49.4 us; the launch traced here: 49 us
  Pallas kernels  47 us (95%)
  between operations  1.93 us (4%)
    pallas_call x1, Pallas kernels, tower(): pl.pallas_call(functools.partial(tower_kernel, n_enc, n_dec, tiles), out_...  44.2 us
    pallas_call x1, Pallas kernels, unpack_all(): pl.pallas_call(functools.partial(unpack_kernel, scale), out_shape=tuple((...  2.82 us

profile of v5, /device:TPU:0, one launch (start us, length us, event | category | flops | bytes accessed | tf_op | source)
XLA Modules:
  0.0 49.0 jit_solution(510291580920004939)
XLA Ops:
  1.9 44.2 %tower.1 = (bf16[208,384]{1,0:T(8,128)(2,1)}, bf16[4608,128]{1,0:T(8,128)(2,1)}, bf16[512,128]{1,0:T(8,128)(2,1)}) custom-call(s32[1,1]{1,0:T(1,128)S(6)} %copy.17.refs_0_, s32[1,1]{1,0:T(1,128)S(6)} %copy.18.refs_1_, bf16[1,9,3072]{2,1,0:T(8,128)(2,1)} %refs_2_.1, bf16[48,384]{1,0:T(8,128)(2,1)} %refs_3_.1, bf16[49,384]{1,0:T(8,128)(2,1)} %refs_4_.1, ...), custom_call_target="tpu_custom_call" | custom-call | tf_op jit(solution)/shard_map/tower/pallas_call | solution.py:612
  46.1 2.8 %unpack.1 = (bf16[1,208,384]{2,1,0:T(8,128)(2,1)}, f32[48,384]{1,0:T(8,128)}, f32[49,384]{1,0:T(8,128)}, f32[384]{0:T(512)}, f32[384,768]{1,0:T(8,128)}, /*index=5*/f32[768,384]{1,0:T(8,128)}, f32[384]{0:T(512)}) custom-call(bf16[208,384]{1,0:T(8,128)(2,1)} %get-tuple-element.10.seq_any, bf16[4608,128]{1,0:T(8,128)(2,1)} %get-tuple-element.11.big_any, ...), custom_call_target="tpu_custom_call" | custom-call | tf_op jit(solution)/shard_map/unpack/pallas_call | solution.py:706
